TPU v7x, 32 devices: a whole 2x2x4 slice. The times are simulated.
32 devices in a mesh: lat: 8 (over z, y), lon: 4 (over x, core).
Axes of the slice: x: 2, y: 2, z: 4, core: 2. Of those that a mesh axis runs over, the one named last changes fastest.
Arguments:
- grid_state: bfloat16 [1, 32, 1024, 1024], P(None, 'lat', 'lon'), may hold values from -45 to 45
- stencil_one: float32 [2, 3, 1024], replicated, may hold values from -1.5 to 1.5
- stencil_two: float32 [2, 3, 1024], replicated, may hold values from -1.5 to 1.5
- norm_gain: float32 [1024], replicated, may hold values from 0.5 to 1.5
- query_weight: bfloat16 [1024, 1024], replicated, may hold values from -0.125 to 0.125
- key_value_weight: bfloat16 [1024, 512], replicated, may hold values from -3.125 to 3.125
Outputs:
- mixed_field: bfloat16 [1, 32, 1024, 1024], P(None, 'lat', 'lon')
- attended: bfloat16 [1, 32, 1024, 1024], P(None, 'lat', 'lon')
All inputs are finite; a program needn't handle non-finite values.
Results may differ from a plain program's by a relative error of at most 0.035.
Values may be sent and summed in bfloat16 or wider, within the bound.
A program may use at most 128 MiB of HBM per device.

v0:
```python
import math

import jax
import jax.numpy as jnp
from jax import lax
from jax.sharding import PartitionSpec as P

HEADS = 16
KV_HEADS = 4
HEAD_DIM = 64


def extended_2(cells, sides, width, closed):
    for axis, dim in sides:
        count = lax.axis_size(axis)
        ends = count if closed else count - 1
        head = lax.slice_in_dim(cells, 0, width, axis=dim)
        tail = lax.slice_in_dim(cells, cells.shape[dim] - width, cells.shape[dim], axis=dim)
        cells = jnp.concatenate(
            [
                lax.ppermute(tail, axis, [(i, (i + 1) % count) for i in range(ends)]),
                cells,
                lax.ppermute(head, axis, [((i + 1) % count, i) for i in range(ends)]),
            ],
            axis=dim,
        )
    return cells


def from_partner(x, axis, distance):
    return lax.ppermute(x, axis, [(i, i ^ 1 << distance) for i in range(lax.axis_size(axis))])


def band_weights(first_row, row_count, nlat_total):
    positions = (jnp.arange(row_count, dtype=jnp.int32) + first_row).astype(jnp.float32)
    return jnp.abs(jnp.sin(jnp.pi * (positions + 0.5) / nlat_total))


def apply_stencil(extended, weights, row_weights):
    scaled = extended.astype(jnp.float32) * row_weights[None, :, None, None]
    column_count = extended.shape[2] - 2
    running = jnp.zeros_like(scaled[:, 1:-1, 1:-1])
    for offset in range(3):
        centre = scaled[:, 1:-1, offset : offset + column_count]
        beside = (
            scaled[:, :-2, offset : offset + column_count]
            + scaled[:, 2:, offset : offset + column_count]
        )
        running = running + weights[0, offset] * centre + weights[1, offset] * beside
    return (extended[:, 1:-1, 1:-1].astype(jnp.float32) + running).astype(jnp.bfloat16)


def place_poles(band_rows, mirrored, margin):
    band_index = lax.axis_index("lat")
    last_band = lax.axis_size("lat") - 1
    upper_rim = jnp.where(band_index == 0, mirrored[:, :margin][:, ::-1], band_rows[:, :margin])
    lower_rim = jnp.where(
        band_index == last_band, mirrored[:, margin:][:, ::-1], band_rows[:, -margin:]
    )
    return jnp.concatenate([upper_rim, band_rows[:, margin:-margin], lower_rim], axis=1)


def extend_once(layer_input):
    band_rows = extended_2(layer_input, (("lat", 1),), 1, False)
    polar_rows = jnp.concatenate([layer_input[:, :1], layer_input[:, -1:]], axis=1)
    mirrored = from_partner(polar_rows, "lon", lax.axis_size("lon").bit_length() - 2)
    band_rows = place_poles(band_rows, mirrored, 1)
    return extended_2(band_rows, (("lon", 2),), 1, True)


def local(grid_state, stencil_one, stencil_two, norm_gain, query_weight, key_value_weight):
    level_count, band_count, lon_count, channels = grid_state.shape
    circles = level_count * band_count
    nlat_total = band_count * lax.axis_size("lat")
    band_start = lax.axis_index("lat") * band_count
    row_weights = band_weights(band_start - 1, band_count + 2, nlat_total)
    after_one = apply_stencil(extend_once(grid_state), stencil_one, row_weights)
    mixed_field = apply_stencil(extend_once(after_one), stencil_two, row_weights)
    flattened = mixed_field.reshape(circles * lon_count, channels).astype(jnp.float32)
    mean_square = jnp.mean(flattened * flattened, axis=-1, keepdims=True)
    normed = (flattened * lax.rsqrt(mean_square + 1e-06) * norm_gain).astype(jnp.bfloat16)
    queries = jnp.dot(normed, query_weight, preferred_element_type=jnp.float32).astype(jnp.bfloat16)
    key_values = jnp.dot(normed, key_value_weight, preferred_element_type=jnp.float32).astype(
        jnp.bfloat16
    )
    key_width = KV_HEADS * HEAD_DIM
    queries = queries.reshape(circles, lon_count, channels)
    key_rows = key_values[:, :key_width].reshape(circles, lon_count, key_width)
    value_rows = key_values[:, key_width:].reshape(circles, lon_count, key_width)
    groups = HEADS // KV_HEADS
    grouped_queries = queries.reshape(circles, lon_count, KV_HEADS, groups, HEAD_DIM)
    start_peak = jnp.full((circles, KV_HEADS, groups, lon_count), -jnp.inf, jnp.float32)
    start_sum = jnp.zeros((circles, KV_HEADS, groups, lon_count), jnp.float32)
    start_acc = jnp.zeros((circles, KV_HEADS, groups, lon_count, HEAD_DIM), jnp.float32)
    key_block = lax.all_gather(key_rows, "lon", axis=1, tiled=True)
    value_block = lax.all_gather(value_rows, "lon", axis=1, tiled=True)
    block_cols = key_block.shape[1]
    key_block = key_block.reshape(circles, block_cols, KV_HEADS, HEAD_DIM)
    value_block = value_block.reshape(circles, block_cols, KV_HEADS, HEAD_DIM)

    def one_band(packed):
        row_peak, denominator, running, query_band, key_band, value_band = packed
        scores = jnp.einsum(
            "wkgd,pkd->kgwp", query_band, key_band, preferred_element_type=jnp.float32
        ) / math.sqrt(HEAD_DIM)
        new_peak = jnp.maximum(row_peak, jnp.max(scores, axis=-1))
        factor = jnp.exp(row_peak - new_peak)
        exponent = jnp.exp(scores - new_peak[..., None])
        denominator = denominator * factor + jnp.sum(exponent, axis=-1)
        update = jnp.einsum(
            "kgwp,pkd->kgwd",
            exponent.astype(jnp.bfloat16),
            value_band,
            preferred_element_type=jnp.float32,
        )
        running = running * factor[..., None] + update
        return (new_peak, denominator, running)

    row_peak, denominator, running = lax.map(
        one_band, (start_peak, start_sum, start_acc, grouped_queries, key_block, value_block)
    )
    mixed = running / denominator[..., None]
    attended = (
        jnp.transpose(mixed, (0, 3, 1, 2, 4))
        .reshape(circles, lon_count, channels)
        .astype(jnp.bfloat16)
    )
    return (mixed_field, attended.reshape(level_count, band_count, lon_count, channels))


def solution(mesh):
    in_specs = (P(None, "lat", "lon", None), P(), P(), P(), P(), P())
    out_specs = (P(None, "lat", "lon", None), P(None, "lat", "lon", None))
    return jax.shard_map(local, mesh=mesh, in_specs=in_specs, out_specs=out_specs, check_vma=False)
```

profile of v0, /device:TPU:25, one launch (start us, length us, event | category | flops | bytes accessed | tf_op | source)
XLA Modules:
  0.0 252.6 jit_solution(15845111107275023811)
XLA Ops:
  17.2 9.2 %collective-permute-done.1 = bf16[1,1,256,1024]{3,2,1,0:T(8,128)(2,1)} collective-permute-done((bf16[1,1,256,1024]{3,2,1,0:T(8,128)(2,1)S(1)}, bf16[1,1,256,1024]{3,2,1,0:T(8,128)(2,1)}, u32[]{:S(2)}, u32[]{:S(2)}) %collective-permute-start.1) | collective-permute-done | bytes 524320 | tf_op jit(solution)/shard_map/ppermute | solution.py:21
  26.3 12.6 %collective-permute-done.2 = bf16[1,1,256,1024]{3,2,1,0:T(8,128)(2,1)} collective-permute-done((bf16[1,1,256,1024]{3,2,1,0:T(8,128)(2,1)S(1)}, bf16[1,1,256,1024]{3,2,1,0:T(8,128)(2,1)}, u32[]{:S(2)}, u32[]{:S(2)}) %collective-permute-start.2) | collective-permute-done | bytes 524320 | tf_op jit(solution)/shard_map/ppermute | solution.py:23
  45.9 5.2 %fusion.37 = bf16[1,4,256,1024]{3,2,1,0:T(8,128)(2,1)S(1)} fusion(f32[1,6,258,1024]{3,2,1,0:T(8,128)S(1)} %convert_multiply_fusion.1, bf16[1,4,256,1024]{3,2,1,0:T(8,128)(2,1)} %param.8, f32[1024]{0:T(1024)S(1)} %bitcast.105, f32[1024]{0:T(1024)S(1)} %bitcast.106, f32[1024]{0:T(1024)S(1)} %bitcast.102, f32[1024]{0:T(1024)S(1)} %bitcast.103, ...), kind=kLoop, calls=%fused_computation.43 | loop fusion | flops 17825792 | bytes 41967616 | tf_op jit(solution)/shard_map/convert_element_type | solution.py:50
  54.6 4.3 %collective-permute-start.7 = (bf16[1,1,256,1024]{3,2,1,0:T(8,128)(2,1)S(1)}, bf16[1,1,256,1024]{3,2,1,0:T(8,128)(2,1)S(1)}, u32[]{:S(2)}, u32[]{:S(2)}) collective-permute-start(bf16[1,1,256,1024]{3,2,1,0:T(8,128)(2,1)S(1)} %get-tuple-element.72), channel_id=1, source_target_pairs={{4,0},{8,4},{12,8},{16,12},{20,16},{24,20},{28,24},{5,1},{9,5},{13... | collective-permute-start | bytes 1572872 | tf_op jit(solution)/shard_map/ppermute | solution.py:23
  58.9 10.0 %collective-permute-done.6 = bf16[1,1,256,1024]{3,2,1,0:T(8,128)(2,1)S(1)} collective-permute-done((bf16[1,1,256,1024]{3,2,1,0:T(8,128)(2,1)S(1)}, bf16[1,1,256,1024]{3,2,1,0:T(8,128)(2,1)S(1)}, u32[]{:S(2)}, u32[]{:S(2)}) %collective-permute-start.6) | collective-permute-done | bytes 524320 | tf_op jit(solution)/shard_map/ppermute | solution.py:21
  68.9 11.4 %collective-permute-done.7 = bf16[1,1,256,1024]{3,2,1,0:T(8,128)(2,1)S(1)} collective-permute-done((bf16[1,1,256,1024]{3,2,1,0:T(8,128)(2,1)S(1)}, bf16[1,1,256,1024]{3,2,1,0:T(8,128)(2,1)S(1)}, u32[]{:S(2)}, u32[]{:S(2)}) %collective-permute-start.7) | collective-permute-done | bytes 524320 | tf_op jit(solution)/shard_map/ppermute | solution.py:23
  86.1 5.4 %multiply_reduce_fusion = (f32[4,256]{1,0:T(4,128)S(1)}, bf16[1,4,256,1024]{3,2,1,0:T(8,128)(2,1)}) fusion(f32[1,6,258,1024]{3,2,1,0:T(8,128)S(1)} %convert_multiply_fusion, f32[1024]{0:T(1024)S(1)} %bitcast.98, f32[1024]{0:T(1024)S(1)} %bitcast.99, f32[1024]{0:T(1024)S(1)} %bitcast.95, f32[1024]{0:T(1024)S(1)} %bitcast.96, f32[1024]{0:T(1024)S(1)} %bitcast.97, ...), kind=kLoop, calls=%fused_computation.59 | loop fusion | flops 20970496 | bytes 41971712 | tf_op jit(solution)/shard_map/reduce_sum | solution.py:80
  96.9 5.3 %convolution_convert_fusion = bf16[1024,1024]{1,0:T(8,128)(2,1)} fusion(bf16[1024,1024]{1,0:T(8,128)(2,1)} %copy-done.4, bf16[1024,1024]{1,0:T(8,128)(2,1)S(1)} %copy-done), kind=kOutput, calls=%fused_computation.60 | convolution fusion | flops 2148532224 | bytes 6291456 | tf_op jit(solution)/shard_map/dot_general | solution.py:82
  102.2 8.5 %reshape.224 = bf16[4,256,4,4,64]{4,3,2,1,0:T(4,128)(2,1)} reshape(bf16[1024,1024]{1,0:T(8,128)(2,1)} %convolution_convert_fusion) | data formatting | bytes 4194304 | tf_op jit(solution)/shard_map/reshape;reshape | solution.py:91
  110.6 7.1 %copy.17 = bf16[4,256,4,4,64]{1,4,3,2,0:T(8,128)(2,1)} copy(bf16[4,256,4,4,64]{4,3,2,1,0:T(4,128)(2,1)} %reshape.224) | data formatting | bytes 4194304 | tf_op jit(solution)/shard_map/while | solution.py:119
  118.4 3.9 %copy.14 = bf16[4,1024,256]{1,2,0:T(8,128)(2,1)} copy(bf16[4,1024,256]{2,1,0:T(8,128)(2,1)} %all-gather.3.cloned.1.call-done) | data formatting | bytes 4194304 | tf_op jit(solution)/shard_map/all_gather | solution.py:95
  122.3 20.2 %all-gather.5.cloned.1.call-done = bf16[4,1024,256]{2,1,0:T(8,128)(2,1)} async-done(((bf16[4,256,256]{2,1,0:T(8,128)(2,1)}), bf16[4,1024,256]{2,1,0:T(8,128)(2,1)}) %all-gather.5.cloned.1.call-update) | async-done | bytes 2097168 | tf_op jit(solution)/shard_map/all_gather | solution.py:96
  142.5 4.0 %copy.16 = bf16[4,1024,256]{1,2,0:T(8,128)(2,1)} copy(bf16[4,1024,256]{2,1,0:T(8,128)(2,1)} %all-gather.5.cloned.1.call-done) | data formatting | bytes 4194304 | tf_op jit(solution)/shard_map/all_gather | solution.py:96
  146.6 91.0 %while.12 = (s32[]{:T(128)}, f32[4,4,4,256]{3,2,1,0:T(4,128)S(1)}, f32[4,4,4,256,64]{3,4,2,1,0:T(8,128)}, bf16[4,1024,4,64]{1,3,2,0:T(8,128)(2,1)}, bf16[4,256,4...) while((s32[]{:T(128)}, f32[4,4,4,256]{3,2,1,0:T(4,128)S(1)}, ...), condition=%wide.region_4.5_spmd, body=%wide.region_1.4_spmd.sunk | while | flops 1107570688 | bytes 120227952 | solution.py:119
  146.6 3.6 %bitcast_reduce_fusion.2 = (f32[4,4,256]{2,1,0:T(4,128)S(1)}, f32[4,1024,256,4]{2,1,3,0:T(8,128)S(1)}) fusion(bf16[4,256,4,4,64]{1,4,3,2,0:T(8,128)(2,1)} %get-tuple-element.152, s32[]{:T(128)} %get-tuple-element.141, bf16[4,1024,4,64]{1,3,2,0:T(8,128)(2,1)} %get-tuple-element.151), kind=kOutput, calls=%fused_computation.1.clone.1 | convolution fusion | flops 545255424 | bytes 17843200 | tf_op jit(solution)/shard_map/while/body/eval_jaxpr/wkgd,pkd->kgwp/dot_general | solution.py:103
  150.2 5.7 %copy-done.2 = f32[4,1024,256,4]{2,1,3,0:T(8,128)} copy-done((f32[4,1024,256,4]{2,1,3,0:T(8,128)}, f32[4,1024,256,4]{2,1,3,0:T(8,128)S(1)}, u32[]{:S(2)}) %copy-start.2) | copy-done | bytes 16777240 | tf_op jit(solution)/shard_map/while
  155.9 4.9 %fusion.63 = f32[4,4,4,256,64]{3,4,2,1,0:T(8,128)} fusion(f32[4,4,4,256,64]{3,4,2,1,0:T(8,128)} %get-tuple-element.143, s32[]{:T(128)} %get-tuple-element.141, f32[4,1024,256,4]{2,1,3,0:T(8,128)S(1)} %get-tuple-element.132, f32[4,4,256]{2,1,0:T(4,128)S(1)} %get-tuple-element.133, bf16[4,1024,4,64]{1,3,2,0:T(8,128)(2,1)} %get-tuple-element.153, ...), kind=kOutput, calls=%fused_computation.8.clone.1 | convolution fusion | flops 549715968 | bytes 18383872 | tf_op jit(solution)/shard_map/while/body/eval_jaxpr/kgwp,pkd->kgwd/dot_general | solution.py:110
  160.8 8.5 %fusion.62 = f32[4,4,256]{2,1,0:T(4,128)S(1)} fusion(f32[4,1024,256,4]{2,1,3,0:T(8,128)} %copy-done.2, f32[4,4,256]{2,1,0:T(4,128)S(1)} %get-tuple-element.133), kind=kLoop, calls=%fused_computation.4.clone.1 | loop fusion | flops 12578816 | bytes 16809984 | tf_op jit(solution)/shard_map/while/body/eval_jaxpr/reduce_sum | solution.py:109
  169.3 3.6 %bitcast_reduce_fusion.2 = (f32[4,4,256]{2,1,0:T(4,128)S(1)}, f32[4,1024,256,4]{2,1,3,0:T(8,128)S(1)}) fusion(bf16[4,256,4,4,64]{1,4,3,2,0:T(8,128)(2,1)} %get-tuple-element.152, s32[]{:T(128)} %get-tuple-element.141, bf16[4,1024,4,64]{1,3,2,0:T(8,128)(2,1)} %get-tuple-element.151), kind=kOutput, calls=%fused_computation.1.clone.1 | convolution fusion | flops 545255424 | bytes 17843200 | tf_op jit(solution)/shard_map/while/body/eval_jaxpr/wkgd,pkd->kgwp/dot_general | solution.py:103
  172.9 5.7 %copy-done.2 = f32[4,1024,256,4]{2,1,3,0:T(8,128)} copy-done((f32[4,1024,256,4]{2,1,3,0:T(8,128)}, f32[4,1024,256,4]{2,1,3,0:T(8,128)S(1)}, u32[]{:S(2)}) %copy-start.2) | copy-done | bytes 16777240 | tf_op jit(solution)/shard_map/while
  178.6 4.9 %fusion.63 = f32[4,4,4,256,64]{3,4,2,1,0:T(8,128)} fusion(f32[4,4,4,256,64]{3,4,2,1,0:T(8,128)} %get-tuple-element.143, s32[]{:T(128)} %get-tuple-element.141, f32[4,1024,256,4]{2,1,3,0:T(8,128)S(1)} %get-tuple-element.132, f32[4,4,256]{2,1,0:T(4,128)S(1)} %get-tuple-element.133, bf16[4,1024,4,64]{1,3,2,0:T(8,128)(2,1)} %get-tuple-element.153, ...), kind=kOutput, calls=%fused_computation.8.clone.1 | convolution fusion | flops 549715968 | bytes 18383872 | tf_op jit(solution)/shard_map/while/body/eval_jaxpr/kgwp,pkd->kgwd/dot_general | solution.py:110
  183.5 8.5 %fusion.62 = f32[4,4,256]{2,1,0:T(4,128)S(1)} fusion(f32[4,1024,256,4]{2,1,3,0:T(8,128)} %copy-done.2, f32[4,4,256]{2,1,0:T(4,128)S(1)} %get-tuple-element.133), kind=kLoop, calls=%fused_computation.4.clone.1 | loop fusion | flops 12578816 | bytes 16809984 | tf_op jit(solution)/shard_map/while/body/eval_jaxpr/reduce_sum | solution.py:109
  192.1 3.6 %bitcast_reduce_fusion.2 = (f32[4,4,256]{2,1,0:T(4,128)S(1)}, f32[4,1024,256,4]{2,1,3,0:T(8,128)S(1)}) fusion(bf16[4,256,4,4,64]{1,4,3,2,0:T(8,128)(2,1)} %get-tuple-element.152, s32[]{:T(128)} %get-tuple-element.141, bf16[4,1024,4,64]{1,3,2,0:T(8,128)(2,1)} %get-tuple-element.151), kind=kOutput, calls=%fused_computation.1.clone.1 | convolution fusion | flops 545255424 | bytes 17843200 | tf_op jit(solution)/shard_map/while/body/eval_jaxpr/wkgd,pkd->kgwp/dot_general | solution.py:103
  195.7 5.7 %copy-done.2 = f32[4,1024,256,4]{2,1,3,0:T(8,128)} copy-done((f32[4,1024,256,4]{2,1,3,0:T(8,128)}, f32[4,1024,256,4]{2,1,3,0:T(8,128)S(1)}, u32[]{:S(2)}) %copy-start.2) | copy-done | bytes 16777240 | tf_op jit(solution)/shard_map/while
  201.4 4.9 %fusion.63 = f32[4,4,4,256,64]{3,4,2,1,0:T(8,128)} fusion(f32[4,4,4,256,64]{3,4,2,1,0:T(8,128)} %get-tuple-element.143, s32[]{:T(128)} %get-tuple-element.141, f32[4,1024,256,4]{2,1,3,0:T(8,128)S(1)} %get-tuple-element.132, f32[4,4,256]{2,1,0:T(4,128)S(1)} %get-tuple-element.133, bf16[4,1024,4,64]{1,3,2,0:T(8,128)(2,1)} %get-tuple-element.153, ...), kind=kOutput, calls=%fused_computation.8.clone.1 | convolution fusion | flops 549715968 | bytes 18383872 | tf_op jit(solution)/shard_map/while/body/eval_jaxpr/kgwp,pkd->kgwd/dot_general | solution.py:110
  206.3 8.5 %fusion.62 = f32[4,4,256]{2,1,0:T(4,128)S(1)} fusion(f32[4,1024,256,4]{2,1,3,0:T(8,128)} %copy-done.2, f32[4,4,256]{2,1,0:T(4,128)S(1)} %get-tuple-element.133), kind=kLoop, calls=%fused_computation.4.clone.1 | loop fusion | flops 12578816 | bytes 16809984 | tf_op jit(solution)/shard_map/while/body/eval_jaxpr/reduce_sum | solution.py:109
  214.8 3.6 %bitcast_reduce_fusion.2 = (f32[4,4,256]{2,1,0:T(4,128)S(1)}, f32[4,1024,256,4]{2,1,3,0:T(8,128)S(1)}) fusion(bf16[4,256,4,4,64]{1,4,3,2,0:T(8,128)(2,1)} %get-tuple-element.152, s32[]{:T(128)} %get-tuple-element.141, bf16[4,1024,4,64]{1,3,2,0:T(8,128)(2,1)} %get-tuple-element.151), kind=kOutput, calls=%fused_computation.1.clone.1 | convolution fusion | flops 545255424 | bytes 17843200 | tf_op jit(solution)/shard_map/while/body/eval_jaxpr/wkgd,pkd->kgwp/dot_general | solution.py:103
  218.4 5.7 %copy-done.2 = f32[4,1024,256,4]{2,1,3,0:T(8,128)} copy-done((f32[4,1024,256,4]{2,1,3,0:T(8,128)}, f32[4,1024,256,4]{2,1,3,0:T(8,128)S(1)}, u32[]{:S(2)}) %copy-start.2) | copy-done | bytes 16777240 | tf_op jit(solution)/shard_map/while
  224.1 4.9 %fusion.63 = f32[4,4,4,256,64]{3,4,2,1,0:T(8,128)} fusion(f32[4,4,4,256,64]{3,4,2,1,0:T(8,128)} %get-tuple-element.143, s32[]{:T(128)} %get-tuple-element.141, f32[4,1024,256,4]{2,1,3,0:T(8,128)S(1)} %get-tuple-element.132, f32[4,4,256]{2,1,0:T(4,128)S(1)} %get-tuple-element.133, bf16[4,1024,4,64]{1,3,2,0:T(8,128)(2,1)} %get-tuple-element.153, ...), kind=kOutput, calls=%fused_computation.8.clone.1 | convolution fusion | flops 549715968 | bytes 18383872 | tf_op jit(solution)/shard_map/while/body/eval_jaxpr/kgwp,pkd->kgwd/dot_general | solution.py:110
  229.0 8.5 %fusion.62 = f32[4,4,256]{2,1,0:T(4,128)S(1)} fusion(f32[4,1024,256,4]{2,1,3,0:T(8,128)} %copy-done.2, f32[4,4,256]{2,1,0:T(4,128)S(1)} %get-tuple-element.133), kind=kLoop, calls=%fused_computation.4.clone.1 | loop fusion | flops 12578816 | bytes 16809984 | tf_op jit(solution)/shard_map/while/body/eval_jaxpr/reduce_sum | solution.py:109
  237.6 4.3 %divide_convert_fusion = bf16[4,4,4,256,64]{3,4,2,1,0:T(8,128)(2,1)} fusion(f32[4,4,4,256,64]{3,4,2,1,0:T(8,128)} %get-tuple-element.35, f32[4,4,4,256]{3,2,1,0:T(4,128)S(1)} %get-tuple-element.36), kind=kLoop, calls=%fused_computation.58 | loop fusion | flops 2097152 | bytes 6356992 | tf_op jit(solution)/shard_map/convert_element_type | solution.py:126
  241.9 3.9 %copy.18 = bf16[1,4,256,1024]{3,2,1,0:T(8,128)(2,1)} copy(bf16[1,4,256,1024]{2,3,1,0:T(8,128)(2,1)} %bitcast.91) | data formatting | bytes 4194304
  (68 shorter events, 32.3 us)
Async XLA Ops:
  7.2 89.7 %copy-start = (bf16[1024,1024]{1,0:T(8,128)(2,1)S(1)}, bf16[1024,1024]{1,0:T(8,128)(2,1)}, u32[]{:S(2)}) copy-start(bf16[1024,1024]{1,0:T(8,128)(2,1)} %param.12) | copy-start | bytes 6291460
  7.2 9.9 %copy-start.5 = (f32[2,3,1024]{2,0,1:T(2,128)S(1)}, f32[2,3,1024]{2,0,1:T(2,128)}, u32[]{:S(2)}) copy-start(f32[2,3,1024]{2,0,1:T(2,128)} %param.9) | copy-start | bytes 73732
  7.2 111.2 %all-gather.3.cloned.1.call-start = ((), (), s32[]{:S(2)}) async-start(), calls=%async_computation | async-start | bytes 2621440 | tf_op jit(solution)/shard_map/all_gather | solution.py:95
  9.7 29.2 %collective-permute-start = (bf16[1,2,256,1024]{3,2,1,0:T(8,128)(2,1)}, bf16[1,2,256,1024]{3,2,1,0:T(8,128)(2,1)}, u32[]{:S(2)}, u32[]{:S(2)}) collective-permute-start(bf16[1,2,256,1024]{3,2,1,0:T(8,128)(2,1)} %pad_maximum_fusion), channel_id=1, source_target_pairs={{0,2},{1,3},{2,0},{3,1},{4,6},{5,7},{6,4},{7,5},{8,10},{9,11},{10,... | collective-permute-start | bytes 3145736 | tf_op jit(solution)/shard_map/ppermute | solution.py:31
  10.9 15.4 %collective-permute-start.1 = (bf16[1,1,256,1024]{3,2,1,0:T(8,128)(2,1)S(1)}, bf16[1,1,256,1024]{3,2,1,0:T(8,128)(2,1)}, u32[]{:S(2)}, u32[]{:S(2)}) collective-permute-start(bf16[1,1,256,1024]{3,2,1,0:T(8,128)(2,1)S(1)} %get-tuple-element.73), channel_id=1, source_target_pairs={{0,4},{4,8},{8,12},{12,16},{16,20},{20,24},{24,28},{1,5},{5,9},{9,... | collective-permute-start | bytes 1572872 | tf_op jit(solution)/shard_map/ppermute | solution.py:21
  14.1 24.8 %collective-permute-start.2 = (bf16[1,1,256,1024]{3,2,1,0:T(8,128)(2,1)S(1)}, bf16[1,1,256,1024]{3,2,1,0:T(8,128)(2,1)}, u32[]{:S(2)}, u32[]{:S(2)}) collective-permute-start(bf16[1,1,256,1024]{3,2,1,0:T(8,128)(2,1)S(1)} %get-tuple-element.74), channel_id=1, source_target_pairs={{4,0},{8,4},{12,8},{16,12},{20,16},{24,20},{28,24},{5,1},{9,5},{13... | collective-permute-start | bytes 1572872 | tf_op jit(solution)/shard_map/ppermute | solution.py:23
  17.1 23.4 %copy-start.3 = (bf16[1,4,256,1024]{3,2,1,0:T(8,128)(2,1)S(1)}, bf16[1,4,256,1024]{3,2,1,0:T(8,128)(2,1)}, u32[]{:S(2)}) copy-start(bf16[1,4,256,1024]{3,2,1,0:T(8,128)(2,1)} %param.8) | copy-start | bytes 6291460
  40.6 1.6 collective-permute-start.3
  41.3 3.3 %collective-permute-start.4 = (bf16[1,6,1,1024]{3,2,1,0:T(2,128)(2,1)S(1)}, bf16[1,6,1,1024]{3,2,1,0:T(2,128)(2,1)S(1)}, u32[]{:S(2)}, u32[]{:S(2)}) collective-permute-start(bf16[1,6,1,1024]{3,2,1,0:T(2,128)(2,1)S(1)} %get-tuple-element.70), channel_id=1, source_target_pairs={{1,0},{2,1},{3,2},{0,3},{5,4},{6,5},{7,6},{4,7},{9,8},{10,9},{11,1... | collective-permute-start | bytes 36872 | tf_op jit(solution)/shard_map/ppermute | solution.py:23
  51.3 30.1 %copy-start.6 = (f32[2,3,1024]{2,0,1:T(2,128)S(1)}, f32[2,3,1024]{2,0,1:T(2,128)}, u32[]{:S(2)}) copy-start(f32[2,3,1024]{2,0,1:T(2,128)} %param.10) | copy-start | bytes 73732
  51.4 28.9 %collective-permute-start.5 = (bf16[1,2,256,1024]{3,2,1,0:T(8,128)(2,1)S(1)}, bf16[1,2,256,1024]{3,2,1,0:T(8,128)(2,1)S(1)}, u32[]{:S(2)}, u32[]{:S(2)}) collective-permute-start(bf16[1,2,256,1024]{3,2,1,0:T(8,128)(2,1)S(1)} %pad_maximum_fusion.1), channel_id=1, source_target_pairs={{0,2},{1,3},{2,0},{3,1},{4,6},{5,7},{6,4},{7,5},{8,10},{9,11},{10,... | collective-permute-start | bytes 3145736 | tf_op jit(solution)/shard_map/ppermute | solution.py:31
  52.7 16.2 %collective-permute-start.6 = (bf16[1,1,256,1024]{3,2,1,0:T(8,128)(2,1)S(1)}, bf16[1,1,256,1024]{3,2,1,0:T(8,128)(2,1)S(1)}, u32[]{:S(2)}, u32[]{:S(2)}) collective-permute-start(bf16[1,1,256,1024]{3,2,1,0:T(8,128)(2,1)S(1)} %get-tuple-element.71), channel_id=1, source_target_pairs={{0,4},{4,8},{8,12},{12,16},{16,20},{20,24},{24,28},{1,5},{5,9},{9,... | collective-permute-start | bytes 1572872 | tf_op jit(solution)/shard_map/ppermute | solution.py:21
  54.6 25.7 %collective-permute-start.7 = (bf16[1,1,256,1024]{3,2,1,0:T(8,128)(2,1)S(1)}, bf16[1,1,256,1024]{3,2,1,0:T(8,128)(2,1)S(1)}, u32[]{:S(2)}, u32[]{:S(2)}) collective-permute-start(bf16[1,1,256,1024]{3,2,1,0:T(8,128)(2,1)S(1)} %get-tuple-element.72), channel_id=1, source_target_pairs={{4,0},{8,4},{12,8},{16,12},{20,16},{24,20},{28,24},{5,1},{9,5},{13... | collective-permute-start | bytes 1572872 | tf_op jit(solution)/shard_map/ppermute | solution.py:23
  80.4 1.9 collective-permute-start.8
  81.4 3.3 %collective-permute-start.9 = (bf16[1,6,1,1024]{3,2,1,0:T(2,128)(2,1)S(1)}, bf16[1,6,1,1024]{3,2,1,0:T(2,128)(2,1)S(1)}, u32[]{:S(2)}, u32[]{:S(2)}) collective-permute-start(bf16[1,6,1,1024]{3,2,1,0:T(2,128)(2,1)S(1)} %get-tuple-element.68), channel_id=1, source_target_pairs={{1,0},{2,1},{3,2},{0,3},{5,4},{6,5},{7,6},{4,7},{9,8},{10,9},{11,1... | collective-permute-start | bytes 36872 | tf_op jit(solution)/shard_map/ppermute | solution.py:23
  86.1 5.4 %copy-start.7 = (f32[1024]{0:T(1024)S(1)}, f32[1024]{0:T(1024)}, u32[]{:S(2)}) copy-start(f32[1024]{0:T(1024)} %param.11) | copy-start | bytes 12292
  91.4 2.3 copy-start.8
  93.7 1.3 copy-start.4
  96.1 46.5 %all-gather.5.cloned.1.call-start = ((), (), s32[]{:S(2)}) async-start(), calls=%async_computation.1 | async-start | bytes 2621440 | tf_op jit(solution)/shard_map/all_gather | solution.py:96
  150.2 5.7 %copy-start.2 = (f32[4,1024,256,4]{2,1,3,0:T(8,128)}, f32[4,1024,256,4]{2,1,3,0:T(8,128)S(1)}, u32[]{:S(2)}) copy-start(f32[4,1024,256,4]{2,1,3,0:T(8,128)S(1)} %get-tuple-element.132) | copy-start | bytes 50331652 | tf_op jit(solution)/shard_map/while
  172.9 5.7 %copy-start.2 = (f32[4,1024,256,4]{2,1,3,0:T(8,128)}, f32[4,1024,256,4]{2,1,3,0:T(8,128)S(1)}, u32[]{:S(2)}) copy-start(f32[4,1024,256,4]{2,1,3,0:T(8,128)S(1)} %get-tuple-element.132) | copy-start | bytes 50331652 | tf_op jit(solution)/shard_map/while
  195.7 5.7 %copy-start.2 = (f32[4,1024,256,4]{2,1,3,0:T(8,128)}, f32[4,1024,256,4]{2,1,3,0:T(8,128)S(1)}, u32[]{:S(2)}) copy-start(f32[4,1024,256,4]{2,1,3,0:T(8,128)S(1)} %get-tuple-element.132) | copy-start | bytes 50331652 | tf_op jit(solution)/shard_map/while
  218.4 5.7 %copy-start.2 = (f32[4,1024,256,4]{2,1,3,0:T(8,128)}, f32[4,1024,256,4]{2,1,3,0:T(8,128)S(1)}, u32[]{:S(2)}) copy-start(f32[4,1024,256,4]{2,1,3,0:T(8,128)S(1)} %get-tuple-element.132) | copy-start | bytes 50331652 | tf_op jit(solution)/shard_map/while
  237.6 8.2 %copy-start.1 = (bf16[1024,1024]{1,0:T(8,128)(2,1)S(1)}, bf16[1024,1024]{1,0:T(8,128)(2,1)}, u32[]{:S(2)}) copy-start(bf16[1024,1024]{1,0:T(8,128)(2,1)} %param.12) | copy-start | bytes 6291460
Sparse Core Ops, SparseCore 0:
  96.2 22.1 all-gather.2
  119.9 22.5 all-gather.4
where the time goes:
time: 255 us; the launch traced here: 253 us
  waiting for transfers between devices  71.2 us (28%)
  other arithmetic  57.2 us (22%)
  local copies, waits for them, and re-layouts  52.8 us (21%)
  matrix products  40.4 us (16%)
  starting transfers between devices  16.6 us (7%)
  between operations  14.3 us (6%)
    reduce_sum x4, other arithmetic, one_band(): denominator = denominator * factor + jnp.sum(exponent, axis=-1)  34 us
    ppermute x4, waiting for transfers between devices, extended_2(): lax.ppermute(head, axis, [((i + 1) % count, i) for i in range(ends)])  28.6 us
    while x8, local copies, waits for them, and re-layouts  22.8 us
    ppermute x4, waiting for transfers between devices, extended_2(): lax.ppermute(tail, axis, [(i, (i + 1) % count) for i in range(ends)])  21 us
    all_gather x1, waiting for transfers between devices, local(): value_block = lax.all_gather(value_rows, 'lon', axis=1, tiled=True)  20.2 us
    dot_general x4, matrix products, one_band(): jnp.einsum('kgwp,pkd->kgwd', exponent.astype(jnp.bfloat16), value_band, p...  19.5 us
    dot_general x4, matrix products, one_band(): jnp.einsum('wkgd,pkd->kgwp', query_band, key_band, preferred_element_type...  14.4 us
    another operation x1, local copies, waits for them, and re-layouts, local(): queries.reshape(circles, lon_count, KV_HEADS, groups, HEAD_DIM)  8.45 us
  transfers between devices with their start and end apart: 12, of which 10 were waited for; matrix products, arithmetic and copies ran while one was open for 10% of the time, Pallas kernels for 0%

commit v1 on v0

--- a/solution.py
+++ b/solution.py
@@ -1,13 +1,103 @@
+import functools
 import math
 
 import jax
 import jax.numpy as jnp
 from jax import lax
+from jax.experimental import pallas as pl
+from jax.experimental.pallas import tpu as pltpu
 from jax.sharding import PartitionSpec as P
 
 HEADS = 16
 KV_HEADS = 4
 HEAD_DIM = 64
+GROUPS = HEADS // KV_HEADS
+BLOCK = KV_HEADS * HEAD_DIM
+QUERY_SCALE = math.log2(math.e) / math.sqrt(HEAD_DIM)
+
+
+def lane_group(shape):
+    return lax.broadcasted_iota(jnp.int32, shape, len(shape) - 1) // HEAD_DIM
+
+
+def place_queries(normed, query_weight_ref, placed_ref):
+    for g in range(KV_HEADS):
+        weight = query_weight_ref[:, g * BLOCK : (g + 1) * BLOCK]
+        block = jnp.dot(normed, weight, preferred_element_type=jnp.float32) * QUERY_SCALE
+        group = lane_group(block.shape)
+        for j in range(GROUPS):
+            shift = (g - j) * HEAD_DIM % BLOCK
+            moved = pltpu.roll(block, shift, 1) if shift else block
+            placed_ref[j, g] = jnp.where(group == g, moved, 0.0).astype(jnp.bfloat16)
+
+
+def attend(placed_ref, keys, values, mixed_ref, store):
+    def one_block(j, carry):
+        mixed = jnp.zeros(mixed_ref.shape[1:], jnp.float32)
+        group = lane_group(mixed.shape)
+        for g in range(KV_HEADS):
+            scores = lax.dot_general(
+                placed_ref[j, g],
+                keys(),
+                (((1,), (1,)), ((), ())),
+                preferred_element_type=jnp.float32,
+            )
+            peak = jnp.max(scores, axis=-1, keepdims=True)
+            probs = jnp.exp2(scores - peak)
+            denominator = jnp.sum(probs, axis=-1, keepdims=True)
+            update = jnp.dot(
+                probs.astype(jnp.bfloat16), values(), preferred_element_type=jnp.float32
+            )
+            mixed = jnp.where(group == g, update / denominator, mixed)
+        mixed_ref[j] = mixed
+        return carry
+
+    lax.fori_loop(0, GROUPS, one_block, 0)
+    for g in range(KV_HEADS):
+        out = jnp.zeros(mixed_ref.shape[1:], jnp.float32)
+        group = lane_group(out.shape)
+        for j in range(GROUPS):
+            shift = (j - g) * HEAD_DIM % BLOCK
+            part = mixed_ref[j]
+            moved = pltpu.roll(part, shift, 1) if shift else part
+            out = jnp.where(group == j, moved, out)
+        store(g, out.astype(jnp.bfloat16))
+
+
+def attention_kernel(normed_ref, key_value_ref, query_weight_ref, out_ref, placed_ref, mixed_ref):
+    place_queries(normed_ref[0], query_weight_ref, placed_ref)
+
+    def store(g, value):
+        out_ref[0, :, g * BLOCK : (g + 1) * BLOCK] = value
+
+    attend(
+        placed_ref,
+        lambda: key_value_ref[0, :, :BLOCK],
+        lambda: key_value_ref[0, :, BLOCK:],
+        mixed_ref,
+        store,
+    )
+
+
+def attention(normed, key_values, query_weight):
+    circles, lon_count, channels = normed.shape
+    columns = key_values.shape[1]
+    return pl.pallas_call(
+        attention_kernel,
+        grid=(circles,),
+        out_shape=jax.ShapeDtypeStruct(normed.shape, jnp.bfloat16),
+        in_specs=[
+            pl.BlockSpec((1, lon_count, channels), lambda i: (i, 0, 0)),
+            pl.BlockSpec((1, columns, 2 * BLOCK), lambda i: (i, 0, 0)),
+            pl.BlockSpec((channels, channels), lambda i: (0, 0)),
+        ],
+        out_specs=pl.BlockSpec((1, lon_count, channels), lambda i: (i, 0, 0)),
+        scratch_shapes=[
+            pltpu.VMEM((GROUPS, KV_HEADS, lon_count, BLOCK), jnp.bfloat16),
+            pltpu.VMEM((GROUPS, lon_count, BLOCK), jnp.float32),
+        ],
+        compiler_params=pltpu.CompilerParams(vmem_limit_bytes=40 * 1024 * 1024),
+    )(normed, key_values, query_weight)
 
 
 def extended_2(cells, sides, width, closed):
@@ -79,52 +169,12 @@
     flattened = mixed_field.reshape(circles * lon_count, channels).astype(jnp.float32)
     mean_square = jnp.mean(flattened * flattened, axis=-1, keepdims=True)
     normed = (flattened * lax.rsqrt(mean_square + 1e-06) * norm_gain).astype(jnp.bfloat16)
-    queries = jnp.dot(normed, query_weight, preferred_element_type=jnp.float32).astype(jnp.bfloat16)
     key_values = jnp.dot(normed, key_value_weight, preferred_element_type=jnp.float32).astype(
         jnp.bfloat16
     )
-    key_width = KV_HEADS * HEAD_DIM
-    queries = queries.reshape(circles, lon_count, channels)
-    key_rows = key_values[:, :key_width].reshape(circles, lon_count, key_width)
-    value_rows = key_values[:, key_width:].reshape(circles, lon_count, key_width)
-    groups = HEADS // KV_HEADS
-    grouped_queries = queries.reshape(circles, lon_count, KV_HEADS, groups, HEAD_DIM)
-    start_peak = jnp.full((circles, KV_HEADS, groups, lon_count), -jnp.inf, jnp.float32)
-    start_sum = jnp.zeros((circles, KV_HEADS, groups, lon_count), jnp.float32)
-    start_acc = jnp.zeros((circles, KV_HEADS, groups, lon_count, HEAD_DIM), jnp.float32)
-    key_block = lax.all_gather(key_rows, "lon", axis=1, tiled=True)
-    value_block = lax.all_gather(value_rows, "lon", axis=1, tiled=True)
-    block_cols = key_block.shape[1]
-    key_block = key_block.reshape(circles, block_cols, KV_HEADS, HEAD_DIM)
-    value_block = value_block.reshape(circles, block_cols, KV_HEADS, HEAD_DIM)
-
-    def one_band(packed):
-        row_peak, denominator, running, query_band, key_band, value_band = packed
-        scores = jnp.einsum(
-            "wkgd,pkd->kgwp", query_band, key_band, preferred_element_type=jnp.float32
-        ) / math.sqrt(HEAD_DIM)
-        new_peak = jnp.maximum(row_peak, jnp.max(scores, axis=-1))
-        factor = jnp.exp(row_peak - new_peak)
-        exponent = jnp.exp(scores - new_peak[..., None])
-        denominator = denominator * factor + jnp.sum(exponent, axis=-1)
-        update = jnp.einsum(
-            "kgwp,pkd->kgwd",
-            exponent.astype(jnp.bfloat16),
-            value_band,
-            preferred_element_type=jnp.float32,
-        )
-        running = running * factor[..., None] + update
-        return (new_peak, denominator, running)
-
-    row_peak, denominator, running = lax.map(
-        one_band, (start_peak, start_sum, start_acc, grouped_queries, key_block, value_block)
-    )
-    mixed = running / denominator[..., None]
-    attended = (
-        jnp.transpose(mixed, (0, 3, 1, 2, 4))
-        .reshape(circles, lon_count, channels)
-        .astype(jnp.bfloat16)
-    )
+    key_values = key_values.reshape(circles, lon_count, 2 * BLOCK)
+    key_values = lax.all_gather(key_values, "lon", axis=1, tiled=True)
+    attended = attention(normed.reshape(circles, lon_count, channels), key_values, query_weight)
     return (mixed_field, attended.reshape(level_count, band_count, lon_count, channels))
 
 

time: 255 us -> 180 us (0.71)
  local copies, waits for them, and re-layouts: 52.8 us -> 6.32 us
  matrix products: 40.4 us -> 2.23 us
  other arithmetic: 57.2 us -> 21.9 us
  Pallas kernels: 0 us -> 35 us
  waiting for transfers between devices: 71.2 us -> 81.8 us
    dot_general x9 -> x0, matrix products: 39.2 us -> none  [the longest x4 19.5 us: one_band(): jnp.einsum('kgwp,pkd->kgwd', exponent.astype(jnp.bfloat16), value_band, p...]
    pallas_call x0 -> x1, Pallas kernels: none -> 35 us  [attention(): pl.pallas_call(attention_kernel, grid=(circles,), out_shape=jax.ShapeDtyp...]
    reduce_sum x4 -> x0, other arithmetic: 34 us -> none  [one_band(): denominator = denominator * factor + jnp.sum(exponent, axis=-1)]
    while x9 -> x0, local copies, waits for them, and re-layouts: 29.8 us -> none
    all_gather x2 -> x1, waiting for transfers between devices: 20.9 us -> 32 us  [local(): key_values = lax.all_gather(key_values, 'lon', axis=1, tiled=True)]
    another operation x1 -> x0, local copies, waits for them, and re-layouts: 8.45 us -> none  [local(): queries.reshape(circles, lon_count, KV_HEADS, groups, HEAD_DIM)]
    all_gather x2 -> x0, local copies, waits for them, and re-layouts: 7.96 us -> none  [the longest x1 4.02 us: local(): value_block = lax.all_gather(value_rows, 'lon', axis=1, tiled=True)]
    convert_element_type x1 -> x0, other arithmetic: 4.28 us -> none  [local(): attended = jnp.transpose(mixed, (0, 3, 1, 2, 4)).reshape(circles, lon_cou...]
  transfers between devices with their start and end apart: 12 -> 11, of which waited for: 10 -> 9; matrix products, arithmetic and copies ran while one was open for 10% -> 1% of each run, Pallas kernels for 0% -> 0%
where the time goes in v1:
time: 180 us; the launch traced here: 178 us
  waiting for transfers between devices  81.8 us (45%)
  Pallas kernels  35 us (19%)
  other arithmetic  21.9 us (12%)
  starting transfers between devices  16.5 us (9%)
  between operations  14.2 us (8%)
  local copies, waits for them, and re-layouts  6.32 us (4%)
  matrix products  2.23 us (1%)
    pallas_call x1, Pallas kernels, attention(): pl.pallas_call(attention_kernel, grid=(circles,), out_shape=jax.ShapeDtyp...  35 us
    all_gather x1, waiting for transfers between devices, local(): key_values = lax.all_gather(key_values, 'lon', axis=1, tiled=True)  32 us
    ppermute x4, waiting for transfers between devices, extended_2(): lax.ppermute(head, axis, [((i + 1) % count, i) for i in range(ends)])  28.6 us
    ppermute x4, waiting for transfers between devices, extended_2(): lax.ppermute(tail, axis, [(i, (i + 1) % count) for i in range(ends)])  21.2 us
    ppermute x4, starting transfers between devices, extended_2(): lax.ppermute(head, axis, [((i + 1) % count, i) for i in range(ends)])  7.3 us
    ppermute x4, starting transfers between devices, extended_2(): lax.ppermute(tail, axis, [(i, (i + 1) % count) for i in range(ends)])  6.69 us
    reduce_sum x1, other arithmetic, local(): mean_square = jnp.mean(flattened * flattened, axis=-1, keepdims=True)  5.36 us
    convert_element_type x1, other arithmetic, apply_stencil(): (extended[:, 1:-1, 1:-1].astype(jnp.float32) + running).astype(jnp.bfloat16)  5.24 us
  transfers between devices with their start and end apart: 11, of which 9 were waited for; matrix products, arithmetic and copies ran while one was open for 1% of the time, Pallas kernels for 0%

profile of v1, /device:TPU:25, one launch (start us, length us, event | category | flops | bytes accessed | tf_op | source)
XLA Modules:
  0.0 178.0 jit_solution(16434318081717258951)
XLA Ops:
  7.2 2.4 %fusion.27 = (bf16[1,1,256,1024]{3,2,1,0:T(8,128)(2,1)}, bf16[1,1,256,1024]{3,2,1,0:T(8,128)(2,1)}) fusion(bf16[1,4,256,1024]{3,2,1,0:T(8,128)(2,1)} %param.6), kind=kLoop, calls=%fused_computation.58 | loop fusion | bytes 2097152 | tf_op jit(solution)/shard_map/slice | solution.py:155
  9.6 2.3 %pad_maximum_fusion = bf16[1,2,256,1024]{3,2,1,0:T(8,128)(2,1)} fusion(bf16[1,1,256,1024]{3,2,1,0:T(8,128)(2,1)} %get-tuple-element.10, bf16[1,1,256,1024]{3,2,1,0:T(8,128)(2,1)} %get-tuple-element.11), kind=kLoop, calls=%fused_computation.42 | loop fusion | flops 524288 | bytes 2097152 | tf_op jit(solution)/shard_map/concatenate | solution.py:155
  11.9 1.2 collective-permute-start
  13.1 3.1 %collective-permute-start.1 = (bf16[1,1,256,1024]{3,2,1,0:T(8,128)(2,1)}, bf16[1,1,256,1024]{3,2,1,0:T(8,128)(2,1)}, u32[]{:S(2)}, u32[]{:S(2)}) collective-permute-start(bf16[1,1,256,1024]{3,2,1,0:T(8,128)(2,1)} %get-tuple-element.10), channel_id=1, source_target_pairs={{0,4},{4,8},{8,12},{12,16},{16,20},{20,24},{24,28},{1,5},{5,9},{9,... | collective-permute-start | bytes 1572872 | tf_op jit(solution)/shard_map/ppermute | solution.py:111
  16.3 3.0 %collective-permute-start.2 = (bf16[1,1,256,1024]{3,2,1,0:T(8,128)(2,1)}, bf16[1,1,256,1024]{3,2,1,0:T(8,128)(2,1)}, u32[]{:S(2)}, u32[]{:S(2)}) collective-permute-start(bf16[1,1,256,1024]{3,2,1,0:T(8,128)(2,1)} %get-tuple-element.11), channel_id=1, source_target_pairs={{4,0},{8,4},{12,8},{16,12},{20,16},{24,20},{28,24},{5,1},{9,5},{13... | collective-permute-start | bytes 1572872 | tf_op jit(solution)/shard_map/ppermute | solution.py:113
  19.4 9.4 %collective-permute-done.1 = bf16[1,1,256,1024]{3,2,1,0:T(8,128)(2,1)} collective-permute-done((bf16[1,1,256,1024]{3,2,1,0:T(8,128)(2,1)}, bf16[1,1,256,1024]{3,2,1,0:T(8,128)(2,1)}, u32[]{:S(2)}, u32[]{:S(2)}) %collective-permute-start.1) | collective-permute-done | bytes 524320 | tf_op jit(solution)/shard_map/ppermute | solution.py:111
  28.7 12.6 %collective-permute-done.2 = bf16[1,1,256,1024]{3,2,1,0:T(8,128)(2,1)} collective-permute-done((bf16[1,1,256,1024]{3,2,1,0:T(8,128)(2,1)}, bf16[1,1,256,1024]{3,2,1,0:T(8,128)(2,1)}, u32[]{:S(2)}, u32[]{:S(2)}) %collective-permute-start.2) | collective-permute-done | bytes 524320 | tf_op jit(solution)/shard_map/ppermute | solution.py:113
  41.3 1.6 slice_select_fusion.3
  43.0 0.7 collective-permute-start.3
  43.7 0.9 collective-permute-done.3
  44.6 2.3 %collective-permute-done.4 = bf16[1,6,1,1024]{3,2,1,0:T(2,128)(2,1)S(1)} collective-permute-done((bf16[1,6,1,1024]{3,2,1,0:T(2,128)(2,1)S(1)}, bf16[1,6,1,1024]{3,2,1,0:T(2,128)(2,1)S(1)}, u32[]{:S(2)}, u32[]{:S(2)}) %collective-permute-start.4) | collective-permute-done | bytes 12320 | tf_op jit(solution)/shard_map/ppermute | solution.py:113
  46.9 1.4 convert_multiply_fusion.1
  48.3 5.2 %fusion.13 = bf16[1,4,256,1024]{3,2,1,0:T(8,128)(2,1)S(1)} fusion(f32[1,6,258,1024]{3,2,1,0:T(8,128)S(1)} %convert_multiply_fusion.1, bf16[1,4,256,1024]{3,2,1,0:T(8,128)(2,1)} %param.6, f32[1024]{0:T(1024)S(1)} %bitcast.44, f32[1024]{0:T(1024)S(1)} %bitcast.45, f32[1024]{0:T(1024)S(1)} %bitcast.41, f32[1024]{0:T(1024)S(1)} %bitcast.42, ...), kind=kLoop, calls=%fused_computation.22 | loop fusion | flops 17825792 | bytes 41967616 | tf_op jit(solution)/shard_map/convert_element_type | solution.py:140
  53.7 0.1 pad_maximum_fusion.1
  53.8 1.3 collective-permute-start.5
  55.1 1.9 %collective-permute-start.6 = (bf16[1,1,256,1024]{3,2,1,0:T(8,128)(2,1)S(1)}, bf16[1,1,256,1024]{3,2,1,0:T(8,128)(2,1)S(1)}, u32[]{:S(2)}, u32[]{:S(2)}) collective-permute-start(bf16[1,1,256,1024]{3,2,1,0:T(8,128)(2,1)S(1)} %get-tuple-element.8), channel_id=1, source_target_pairs={{0,4},{4,8},{8,12},{12,16},{16,20},{20,24},{24,28},{1,5},{5,9},{9,... | collective-permute-start | bytes 1572872 | tf_op jit(solution)/shard_map/ppermute | solution.py:111
  57.0 4.3 %collective-permute-start.7 = (bf16[1,1,256,1024]{3,2,1,0:T(8,128)(2,1)S(1)}, bf16[1,1,256,1024]{3,2,1,0:T(8,128)(2,1)S(1)}, u32[]{:S(2)}, u32[]{:S(2)}) collective-permute-start(bf16[1,1,256,1024]{3,2,1,0:T(8,128)(2,1)S(1)} %get-tuple-element.9), channel_id=1, source_target_pairs={{4,0},{8,4},{12,8},{16,12},{20,16},{24,20},{28,24},{5,1},{9,5},{13... | collective-permute-start | bytes 1572872 | tf_op jit(solution)/shard_map/ppermute | solution.py:113
  61.3 10.0 %collective-permute-done.6 = bf16[1,1,256,1024]{3,2,1,0:T(8,128)(2,1)S(1)} collective-permute-done((bf16[1,1,256,1024]{3,2,1,0:T(8,128)(2,1)S(1)}, bf16[1,1,256,1024]{3,2,1,0:T(8,128)(2,1)S(1)}, u32[]{:S(2)}, u32[]{:S(2)}) %collective-permute-start.6) | collective-permute-done | bytes 524320 | tf_op jit(solution)/shard_map/ppermute | solution.py:111
  71.3 11.4 %collective-permute-done.7 = bf16[1,1,256,1024]{3,2,1,0:T(8,128)(2,1)S(1)} collective-permute-done((bf16[1,1,256,1024]{3,2,1,0:T(8,128)(2,1)S(1)}, bf16[1,1,256,1024]{3,2,1,0:T(8,128)(2,1)S(1)}, u32[]{:S(2)}, u32[]{:S(2)}) %collective-permute-start.7) | collective-permute-done | bytes 524320 | tf_op jit(solution)/shard_map/ppermute | solution.py:113
  82.7 0.1 slice_select_fusion.1
  82.8 1.0 collective-permute-start.8
  83.8 0.9 collective-permute-done.8
  84.7 2.3 %collective-permute-done.9 = bf16[1,6,1,1024]{3,2,1,0:T(2,128)(2,1)S(1)} collective-permute-done((bf16[1,6,1,1024]{3,2,1,0:T(2,128)(2,1)S(1)}, bf16[1,6,1,1024]{3,2,1,0:T(2,128)(2,1)S(1)}, u32[]{:S(2)}, u32[]{:S(2)}) %collective-permute-start.9) | collective-permute-done | bytes 12320 | tf_op jit(solution)/shard_map/ppermute | solution.py:113
  87.0 1.4 convert_multiply_fusion
  88.5 5.4 %multiply_reduce_fusion = (f32[4,256]{1,0:T(4,128)S(1)}, bf16[1,4,256,1024]{3,2,1,0:T(8,128)(2,1)}) fusion(f32[1,6,258,1024]{3,2,1,0:T(8,128)S(1)} %convert_multiply_fusion, f32[1024]{0:T(1024)S(1)} %bitcast.37, f32[1024]{0:T(1024)S(1)} %bitcast.38, f32[1024]{0:T(1024)S(1)} %bitcast.34, f32[1024]{0:T(1024)S(1)} %bitcast.35, f32[1024]{0:T(1024)S(1)} %bitcast.36, ...), kind=kLoop, calls=%fused_computation.40 | loop fusion | flops 20970496 | bytes 41971712 | tf_op jit(solution)/shard_map/reduce_sum | solution.py:170
  93.9 2.1 %fusion.21 = bf16[1024,1024]{1,0:T(8,128)(2,1)S(1)} fusion(bf16[1,4,256,1024]{3,2,1,0:T(8,128)(2,1)} %get-tuple-element.3, f32[1024]{0:T(1024)S(1)} %copy-done.7, f32[1024]{0:T(1024)S(1)} %bitcast.39), kind=kLoop, calls=%fused_computation.36 | loop fusion | flops 4194304 | bytes 4202496 | tf_op jit(solution)/shard_map/convert_element_type | solution.py:171
  96.0 2.2 %convolution_convert_fusion = bf16[1024,512]{1,0:T(8,128)(2,1)} fusion(bf16[1024,1024]{1,0:T(8,128)(2,1)S(1)} %fusion.21, bf16[1024,512]{1,0:T(8,128)(2,1)S(1)} %copy-done), kind=kOutput, calls=%fused_computation.41 | convolution fusion | flops 1074266112 | bytes 4194304 | tf_op jit(solution)/shard_map/dot_general | solution.py:172
  98.3 2.1 %fusion.23.normed_ref = bf16[4,256,1024]{2,1,0:T(8,128)(2,1)S(1)} fusion(bf16[1,4,256,1024]{3,2,1,0:T(8,128)(2,1)} %get-tuple-element.3, f32[1024]{0:T(1024)S(1)} %copy-done.7, f32[4,256]{1,0:T(4,128)S(1)} %get-tuple-element.29), kind=kLoop, calls=%fused_computation.39 | loop fusion | flops 4194304 | bytes 4202496 | tf_op jit(solution)/shard_map/convert_element_type | solution.py:171
  100.4 32.0 %all-gather.2.cloned.1.call-done.key_value_ref = bf16[4,1024,512]{2,1,0:T(8,128)(2,1)} async-done(((bf16[4,256,512]{2,1,0:T(8,128)(2,1)}), bf16[4,1024,512]{2,1,0:T(8,128)(2,1)}) %all-gather.2.cloned.1.call-update) | async-done | bytes 4194320 | tf_op jit(solution)/shard_map/all_gather | solution.py:176
  132.4 2.2 %copy-done.1 = bf16[4,1024,512]{2,1,0:T(8,128)(2,1)S(1)} copy-done((bf16[4,1024,512]{2,1,0:T(8,128)(2,1)S(1)}, bf16[4,1024,512]{2,1,0:T(8,128)(2,1)}, u32[]{:S(2)}) %copy-start.1) | copy-done | bytes 4194328
  134.6 1.6 copy-done.2
  136.2 35.0 %shard_map.77 = bf16[4,256,1024]{2,1,0:T(8,128)(2,1)} custom-call(bf16[4,256,1024]{2,1,0:T(8,128)(2,1)S(1)} %fusion.23.normed_ref, bf16[4,1024,512]{2,1,0:T(8,128)(2,1)S(1)} %copy-done.1, bf16[1024,1024]{1,0:T(8,128)(2,1)S(1)} %copy-done.2), custom_call_target="tpu_custom_call" | custom-call | tf_op jit(solution)/shard_map/pallas_call | solution.py:85
  (28 shorter events, 0.4 us)
Async XLA Ops:
  7.2 88.8 %copy-start = (bf16[1024,512]{1,0:T(8,128)(2,1)S(1)}, bf16[1024,512]{1,0:T(8,128)(2,1)}, u32[]{:S(2)}) copy-start(bf16[1024,512]{1,0:T(8,128)(2,1)} %param.11) | copy-start | bytes 3145732
  7.2 35.7 %copy-start.3 = (bf16[1,4,256,1024]{3,2,1,0:T(8,128)(2,1)S(1)}, bf16[1,4,256,1024]{3,2,1,0:T(8,128)(2,1)}, u32[]{:S(2)}) copy-start(bf16[1,4,256,1024]{3,2,1,0:T(8,128)(2,1)} %param.6) | copy-start | bytes 6291460
  7.2 12.1 %copy-start.5 = (f32[2,3,1024]{2,0,1:T(2,128)S(1)}, f32[2,3,1024]{2,0,1:T(2,128)}, u32[]{:S(2)}) copy-start(f32[2,3,1024]{2,0,1:T(2,128)} %param.7) | copy-start | bytes 73732
  7.2 125.2 %all-gather.2.cloned.1.call-start = ((), (), s32[]{:S(2)}) async-start(), calls=%async_computation | async-start | bytes 5242880 | tf_op jit(solution)/shard_map/all_gather | solution.py:176
  11.9 29.4 %collective-permute-start = (bf16[1,2,256,1024]{3,2,1,0:T(8,128)(2,1)}, bf16[1,2,256,1024]{3,2,1,0:T(8,128)(2,1)}, u32[]{:S(2)}, u32[]{:S(2)}) collective-permute-start(bf16[1,2,256,1024]{3,2,1,0:T(8,128)(2,1)} %pad_maximum_fusion), channel_id=1, source_target_pairs={{0,2},{1,3},{2,0},{3,1},{4,6},{5,7},{6,4},{7,5},{8,10},{9,11},{10,... | collective-permute-start | bytes 3145736 | tf_op jit(solution)/shard_map/ppermute | solution.py:121
  13.1 15.6 %collective-permute-start.1 = (bf16[1,1,256,1024]{3,2,1,0:T(8,128)(2,1)}, bf16[1,1,256,1024]{3,2,1,0:T(8,128)(2,1)}, u32[]{:S(2)}, u32[]{:S(2)}) collective-permute-start(bf16[1,1,256,1024]{3,2,1,0:T(8,128)(2,1)} %get-tuple-element.10), channel_id=1, source_target_pairs={{0,4},{4,8},{8,12},{12,16},{16,20},{20,24},{24,28},{1,5},{5,9},{9,... | collective-permute-start | bytes 1572872 | tf_op jit(solution)/shard_map/ppermute | solution.py:111
  16.3 25.0 %collective-permute-start.2 = (bf16[1,1,256,1024]{3,2,1,0:T(8,128)(2,1)}, bf16[1,1,256,1024]{3,2,1,0:T(8,128)(2,1)}, u32[]{:S(2)}, u32[]{:S(2)}) collective-permute-start(bf16[1,1,256,1024]{3,2,1,0:T(8,128)(2,1)} %get-tuple-element.11), channel_id=1, source_target_pairs={{4,0},{8,4},{12,8},{16,12},{20,16},{24,20},{28,24},{5,1},{9,5},{13... | collective-permute-start | bytes 1572872 | tf_op jit(solution)/shard_map/ppermute | solution.py:113
  19.3 27.6 %copy-start.4 = (bf16[1,4,256,1024]{3,2,1,0:T(8,128)(2,1)S(1)}, bf16[1,4,256,1024]{3,2,1,0:T(8,128)(2,1)}, u32[]{:S(2)}) copy-start(bf16[1,4,256,1024]{3,2,1,0:T(8,128)(2,1)} %param.6) | copy-start | bytes 6291460
  43.0 1.6 collective-permute-start.3
  43.7 3.3 %collective-permute-start.4 = (bf16[1,6,1,1024]{3,2,1,0:T(2,128)(2,1)S(1)}, bf16[1,6,1,1024]{3,2,1,0:T(2,128)(2,1)S(1)}, u32[]{:S(2)}, u32[]{:S(2)}) collective-permute-start(bf16[1,6,1,1024]{3,2,1,0:T(2,128)(2,1)S(1)} %get-tuple-element.7), channel_id=1, source_target_pairs={{1,0},{2,1},{3,2},{0,3},{5,4},{6,5},{7,6},{4,7},{9,8},{10,9},{11,1... | collective-permute-start | bytes 36872 | tf_op jit(solution)/shard_map/ppermute | solution.py:113
  53.7 30.1 %copy-start.6 = (f32[2,3,1024]{2,0,1:T(2,128)S(1)}, f32[2,3,1024]{2,0,1:T(2,128)}, u32[]{:S(2)}) copy-start(f32[2,3,1024]{2,0,1:T(2,128)} %param.8) | copy-start | bytes 73732
  53.8 28.9 %collective-permute-start.5 = (bf16[1,2,256,1024]{3,2,1,0:T(8,128)(2,1)S(1)}, bf16[1,2,256,1024]{3,2,1,0:T(8,128)(2,1)S(1)}, u32[]{:S(2)}, u32[]{:S(2)}) collective-permute-start(bf16[1,2,256,1024]{3,2,1,0:T(8,128)(2,1)S(1)} %pad_maximum_fusion.1), channel_id=1, source_target_pairs={{0,2},{1,3},{2,0},{3,1},{4,6},{5,7},{6,4},{7,5},{8,10},{9,11},{10,... | collective-permute-start | bytes 3145736 | tf_op jit(solution)/shard_map/ppermute | solution.py:121
  55.1 16.2 %collective-permute-start.6 = (bf16[1,1,256,1024]{3,2,1,0:T(8,128)(2,1)S(1)}, bf16[1,1,256,1024]{3,2,1,0:T(8,128)(2,1)S(1)}, u32[]{:S(2)}, u32[]{:S(2)}) collective-permute-start(bf16[1,1,256,1024]{3,2,1,0:T(8,128)(2,1)S(1)} %get-tuple-element.8), channel_id=1, source_target_pairs={{0,4},{4,8},{8,12},{12,16},{16,20},{20,24},{24,28},{1,5},{5,9},{9,... | collective-permute-start | bytes 1572872 | tf_op jit(solution)/shard_map/ppermute | solution.py:111
  57.0 25.7 %collective-permute-start.7 = (bf16[1,1,256,1024]{3,2,1,0:T(8,128)(2,1)S(1)}, bf16[1,1,256,1024]{3,2,1,0:T(8,128)(2,1)S(1)}, u32[]{:S(2)}, u32[]{:S(2)}) collective-permute-start(bf16[1,1,256,1024]{3,2,1,0:T(8,128)(2,1)S(1)} %get-tuple-element.9), channel_id=1, source_target_pairs={{4,0},{8,4},{12,8},{16,12},{20,16},{24,20},{28,24},{5,1},{9,5},{13... | collective-permute-start | bytes 1572872 | tf_op jit(solution)/shard_map/ppermute | solution.py:113
  82.8 1.9 %collective-permute-start.8 = (bf16[1,6,1,1024]{3,2,1,0:T(2,128)(2,1)S(1)}, bf16[1,6,1,1024]{3,2,1,0:T(2,128)(2,1)S(1)}, u32[]{:S(2)}, u32[]{:S(2)}) collective-permute-start(bf16[1,6,1,1024]{3,2,1,0:T(2,128)(2,1)S(1)} %get-tuple-element.4), channel_id=1, source_target_pairs={{0,1},{1,2},{2,3},{3,0},{4,5},{5,6},{6,7},{7,4},{8,9},{9,10},{10,1... | collective-permute-start | bytes 36872 | tf_op jit(solution)/shard_map/ppermute | solution.py:111
  83.8 3.3 %collective-permute-start.9 = (bf16[1,6,1,1024]{3,2,1,0:T(2,128)(2,1)S(1)}, bf16[1,6,1,1024]{3,2,1,0:T(2,128)(2,1)S(1)}, u32[]{:S(2)}, u32[]{:S(2)}) collective-permute-start(bf16[1,6,1,1024]{3,2,1,0:T(2,128)(2,1)S(1)} %get-tuple-element.5), channel_id=1, source_target_pairs={{1,0},{2,1},{3,2},{0,3},{5,4},{6,5},{7,6},{4,7},{9,8},{10,9},{11,1... | collective-permute-start | bytes 36872 | tf_op jit(solution)/shard_map/ppermute | solution.py:113
  88.5 5.4 %copy-start.7 = (f32[1024]{0:T(1024)S(1)}, f32[1024]{0:T(1024)}, u32[]{:S(2)}) copy-start(f32[1024]{0:T(1024)} %param.9) | copy-start | bytes 12292
  132.4 2.2 %copy-start.1 = (bf16[4,1024,512]{2,1,0:T(8,128)(2,1)S(1)}, bf16[4,1024,512]{2,1,0:T(8,128)(2,1)}, u32[]{:S(2)}) copy-start(bf16[4,1024,512]{2,1,0:T(8,128)(2,1)} %all-gather.2.cloned.1.call-done.key_value_ref) | copy-start | bytes 12582916
  134.6 1.6 copy-start.2
Sparse Core Ops, SparseCore 0:
  98.4 34.0 all-gather.1

commit v2 on v1

v2 whole, which is shorter than its diff:
```python
import functools
import math

import jax
import jax.numpy as jnp
from jax import lax
from jax.experimental import pallas as pl
from jax.experimental.pallas import tpu as pltpu
from jax.sharding import PartitionSpec as P

HEADS = 16
KV_HEADS = 4
HEAD_DIM = 64
GROUPS = HEADS // KV_HEADS
BLOCK = KV_HEADS * HEAD_DIM
EDGE = 16
MESH = pl.DeviceIdType.MESH
QUERY_SCALE = math.log2(math.e) / math.sqrt(HEAD_DIM)


def lane_group(shape):
    return lax.broadcasted_iota(jnp.int32, shape, len(shape) - 1) // HEAD_DIM


def place_queries(normed, query_weight_ref, placed_ref):
    for g in range(KV_HEADS):
        weight = query_weight_ref[:, g * BLOCK : (g + 1) * BLOCK]
        block = jnp.dot(normed, weight, preferred_element_type=jnp.float32) * QUERY_SCALE
        group = lane_group(block.shape)
        for j in range(GROUPS):
            shift = (g - j) * HEAD_DIM % BLOCK
            moved = pltpu.roll(block, shift, 1) if shift else block
            placed_ref[j, g] = jnp.where(group == g, moved, 0.0).astype(jnp.bfloat16)


def attend(placed_ref, keys, values, mixed_ref, store):
    def one_block(j, carry):
        mixed = jnp.zeros(mixed_ref.shape[1:], jnp.float32)
        group = lane_group(mixed.shape)
        for g in range(KV_HEADS):
            scores = lax.dot_general(
                placed_ref[j, g],
                keys(),
                (((1,), (1,)), ((), ())),
                preferred_element_type=jnp.float32,
            )
            peak = jnp.max(scores, axis=-1, keepdims=True)
            probs = jnp.exp2(scores - peak)
            denominator = jnp.sum(probs, axis=-1, keepdims=True)
            update = jnp.dot(
                probs.astype(jnp.bfloat16), values(), preferred_element_type=jnp.float32
            )
            mixed = jnp.where(group == g, update / denominator, mixed)
        mixed_ref[j] = mixed
        return carry

    lax.fori_loop(0, GROUPS, one_block, 0)
    for g in range(KV_HEADS):
        out = jnp.zeros(mixed_ref.shape[1:], jnp.float32)
        group = lane_group(out.shape)
        for j in range(GROUPS):
            shift = (j - g) * HEAD_DIM % BLOCK
            part = mixed_ref[j]
            moved = pltpu.roll(part, shift, 1) if shift else part
            out = jnp.where(group == j, moved, out)
        store(g, out.astype(jnp.bfloat16))

def row_weights(first_row, row_count, nlat_total):
    positions = (jnp.arange(row_count, dtype=jnp.int32) + first_row).astype(jnp.float32)
    return jnp.abs(jnp.sin(jnp.pi * (positions + 0.5) / nlat_total))


def block_kernel(
    lat_size,
    lon_size,
    circle_ref,
    grid_ref,
    stencil_one_ref,
    stencil_two_ref,
    gain_ref,
    query_hbm,
    key_value_hbm,
    mixed_out,
    attended_out,
    wide,
    after_one,
    mixed_field,
    normed,
    key_values,
    placed,
    mixed,
    attended,
    query_weight,
    key_value_weight,
    local_sem,
    out_sem,
    halo_send,
    halo_recv,
    side_send,
    side_recv,
    edge_send,
    edge_recv,
    kv_send,
    kv_recv,
):
    band, width, channels = grid_ref.shape
    last = band - 1
    lat = lax.axis_index("lat")
    lon = lax.axis_index("lon")
    chips = lon_size // 2
    left, right = lax.rem(lon + lon_size - 1, lon_size), lax.rem(lon + 1, lon_size)
    sibling = lon + 1 - 2 * lax.rem(lon, 2)
    partner = lax.rem(lon + lon_size // 2, lon_size)
    at_top, at_bottom = lat == 0, lat == lat_size - 1
    top = (jnp.where(at_top, lat, lat - 1), jnp.where(at_top, partner, lon))
    bottom = (jnp.where(at_bottom, lat, lat + 1), jnp.where(at_bottom, partner, lon))

    def remote(src, dst, send, recv, device):
        return pltpu.make_async_remote_copy(
            src_ref=src,
            dst_ref=dst,
            send_sem=send,
            recv_sem=recv,
            device_id=device,
            device_id_type=MESH,
        )

    loads = [
        pltpu.make_async_copy(
            grid_ref, wide.at[pl.ds(2, band), pl.ds(EDGE, width)], local_sem.at[0]
        ),
        pltpu.make_async_copy(key_value_hbm, key_value_weight, local_sem.at[1]),
        pltpu.make_async_copy(query_hbm, query_weight, local_sem.at[2]),
    ]
    for load in loads:
        load.start()

    barrier = pltpu.get_barrier_semaphore()
    for device in (top, bottom):
        pl.semaphore_signal(barrier, inc=1, device_id=device, device_id_type=MESH)
    for step in range(1, lon_size):
        other = (lat, lax.rem(lon + step, lon_size))
        pl.semaphore_signal(barrier, inc=1, device_id=other, device_id_type=MESH)
    pl.semaphore_wait(barrier, lon_size + 1)

    def halo(row, target, device, slot):
        return remote(
            grid_ref.at[row],
            wide.at[target, pl.ds(EDGE, width)],
            halo_send.at[slot],
            halo_recv.at[target],
            device,
        )

    near_top = halo(0, jnp.where(at_top, 1, band + 2), top, 0)
    near_bottom = halo(last, jnp.where(at_bottom, band + 2, 1), bottom, 1)
    far_top = halo(1, jnp.where(at_top, 0, band + 3), top, 2)
    far_bottom = halo(last - 1, jnp.where(at_bottom, band + 3, 0), bottom, 3)
    sides = [
        remote(
            grid_ref.at[:, pl.ds(width - EDGE, EDGE)],
            wide.at[pl.ds(2, band), pl.ds(0, EDGE)],
            side_send.at[0],
            side_recv.at[0],
            (lat, right),
        ),
        remote(
            grid_ref.at[:, pl.ds(0, EDGE)],
            wide.at[pl.ds(2, band), pl.ds(EDGE + width, EDGE)],
            side_send.at[1],
            side_recv.at[1],
            (lat, left),
        ),
    ]
    near_top.start()
    near_bottom.start()
    for side in sides:
        side.start()
    near_top.wait_send()
    far_top.start()
    near_bottom.wait_send()
    far_bottom.start()

    def edges(row):
        slot = {0: 0, 1: 1, band + 2: 2, band + 3: 3}[row]
        return [
            remote(
                wide.at[row, pl.ds(width, EDGE)],
                wide.at[row, pl.ds(0, EDGE)],
                edge_send.at[slot, 0],
                edge_recv.at[slot, 0],
                (lat, right),
            ),
            remote(
                wide.at[row, pl.ds(EDGE, EDGE)],
                wide.at[row, pl.ds(EDGE + width, EDGE)],
                edge_send.at[slot, 1],
                edge_recv.at[slot, 1],
                (lat, left),
            ),
        ]

    def receive_halos(rows):
        for row in rows:
            halo(0, row, top, 0).wait_recv()
            for edge in edges(row):
                edge.start()
        for row in rows:
            for edge in edges(row):
                edge.wait_recv()

    def stencil(source, first, step, count, circle_first, weights_ref, store):
        total = width + 2 * EDGE
        chunks = channels // 128

        def one(index, carry):
            row = first + index // chunks * step
            circle = circle_first + index // chunks * step
            lanes = pl.ds(pl.multiple_of(index % chunks * 128, 128), 128)
            above = source[row - 1, :, lanes].astype(jnp.float32)
            centre = source[row, :, lanes].astype(jnp.float32)
            below = source[row + 1, :, lanes].astype(jnp.float32)
            beside = circle_ref[circle - 1] * above + circle_ref[circle + 1] * below
            own = weights_ref[0, :, lanes] * circle_ref[circle]
            next_to = weights_ref[1, :, lanes]
            result = centre + own[1:2] * centre + next_to[1:2] * beside
            result = result + pltpu.roll(own[0:1] * centre + next_to[0:1] * beside, 1, 0)
            result = result + pltpu.roll(own[2:3] * centre + next_to[2:3] * beside, total - 1, 0)
            store(row, lanes, result.astype(jnp.bfloat16))
            return carry

        lax.fori_loop(0, count * chunks, one, 0)

    def store_after_one(row, lanes, value):
        after_one[row - 1, :, lanes] = value

    def store_mixed(row, lanes, value):
        mixed_field[row - 1, :, lanes] = value[EDGE : EDGE + width]

    def own_columns(owner):
        return pl.ds(pl.multiple_of(owner * width, EDGE), width)

    def kv_copy(row, owner, device, slot):
        block = key_values.at[row, own_columns(owner)]
        return remote(block, block, kv_send.at[row, slot], kv_recv.at[row, owner], device)

    def kv_start(row):
        for step in range(1, chips):
            other = lax.rem(lon + 2 * step, lon_size)
            kv_copy(row, lon, (lat, other), step).start()
        kv_copy(row, lon, (lat, sibling), 0).start()

    def kv_forward(row):
        for step in range(1, chips):
            owner = lax.rem(lon + lon_size - 2 * step, lon_size)
            kv_copy(row, owner, (lat, sibling), 0).wait_recv()
            kv_copy(row, owner, (lat, sibling), chips - 1 + step).start()

    def kv_collect(row):
        for step in range(chips):
            owner = lax.rem(sibling + lon_size - 2 * step, lon_size)
            kv_copy(row, owner, (lat, sibling), 0).wait_recv()

    def mixed_copy(row):
        return pltpu.make_async_copy(mixed_field.at[row], mixed_out.at[row], out_sem.at[0, row])

    def attended_copy(row):
        return pltpu.make_async_copy(attended.at[row], attended_out.at[row], out_sem.at[1, row])

    def project(first, step, count):
        def one(index, carry):
            row = first + index * step
            tokens = mixed_field[row].astype(jnp.float32)
            mean_square = jnp.mean(tokens * tokens, axis=-1, keepdims=True)
            scaled = tokens * lax.rsqrt(mean_square + 1e-06) * gain_ref[...]
            normed[row] = scaled.astype(jnp.bfloat16)
            key_values[row, own_columns(lon)] = jnp.dot(
                normed[row], key_value_weight[...], preferred_element_type=jnp.float32
            ).astype(jnp.bfloat16)
            kv_start(row)
            mixed_copy(row).start()
            return carry

        lax.fori_loop(0, count, one, 0)

    def attend_row(row):
        place_queries(normed[row], query_weight, placed)
        kv_collect(row)

        def store(g, value):
            attended[row, :, g * BLOCK : (g + 1) * BLOCK] = value

        attend(
            placed,
            lambda: key_values[row, :, :BLOCK],
            lambda: key_values[row, :, BLOCK:],
            mixed,
            store,
        )
        attended_copy(row).start()

    loads[0].wait()
    for side in sides:
        side.wait_recv()
    receive_halos((1, band + 2))
    stencil(wide, 2, 1, band, 2, stencil_one_ref, store_after_one)
    loads[1].wait()
    stencil(after_one, 2, 1, band - 2, 3, stencil_two_ref, store_mixed)
    project(1, 1, band - 2)
    loads[2].wait()
    kv_forward(1)
    attend_row(1)

    receive_halos((0, band + 3))
    stencil(wide, 1, band + 1, 2, 1, stencil_one_ref, store_after_one)
    stencil(after_one, 1, last, 2, 2, stencil_two_ref, store_mixed)
    project(0, last, 2)
    kv_forward(2)

    def one_row(index, carry):
        attend_row(lax.rem(index + 2, band))

        @pl.when(index < band - 2)
        def _():
            kv_forward(lax.rem(index + 3, band))

        return carry

    lax.fori_loop(0, band - 1, one_row, 0)

    far_top.wait_send()
    far_bottom.wait_send()
    for side in sides:
        side.wait_send()
    for row in (0, 1, band + 2, band + 3):
        for edge in edges(row):
            edge.wait_send()

    def finish(row, carry):
        for slot in range(lon_size - 1):
            kv_copy(row, lon, (lat, sibling), slot).wait_send()
        mixed_copy(row).wait()
        attended_copy(row).wait()
        return carry

    lax.fori_loop(0, band, finish, 0)


def local(grid_state, stencil_one, stencil_two, norm_gain, query_weight, key_value_weight):
    level_count, band, width, channels = grid_state.shape
    lat_size, lon_size = lax.axis_size("lat"), lax.axis_size("lon")
    circle = row_weights(lax.axis_index("lat") * band - 2, band + 4, band * lat_size)
    whole = pl.BlockSpec(memory_space=pltpu.VMEM)
    anywhere = pl.BlockSpec(memory_space=pl.ANY)
    field = jax.ShapeDtypeStruct((band, width, channels), jnp.bfloat16)
    wide_width = width + 2 * EDGE
    rows = (band, width, channels)
    dma = pltpu.SemaphoreType.DMA
    mixed_field, attended = pl.pallas_call(
        functools.partial(block_kernel, lat_size, lon_size),
        out_shape=(field, field),
        in_specs=[
            pl.BlockSpec(memory_space=pltpu.SMEM),
            anywhere,
            whole,
            whole,
            whole,
            anywhere,
            anywhere,
        ],
        out_specs=(anywhere, anywhere),
        scratch_shapes=[
            pltpu.VMEM((band + 4, wide_width, channels), jnp.bfloat16),
            pltpu.VMEM((band + 2, wide_width, channels), jnp.bfloat16),
            pltpu.VMEM(rows, jnp.bfloat16),
            pltpu.VMEM(rows, jnp.bfloat16),
            pltpu.VMEM((band, width * lon_size, 2 * BLOCK), jnp.bfloat16),
            pltpu.VMEM((GROUPS, KV_HEADS, width, BLOCK), jnp.bfloat16),
            pltpu.VMEM((GROUPS, width, BLOCK), jnp.float32),
            pltpu.VMEM(rows, jnp.bfloat16),
            pltpu.VMEM(query_weight.shape, jnp.bfloat16),
            pltpu.VMEM(key_value_weight.shape, jnp.bfloat16),
            dma((3,)),
            dma((2, band)),
            dma((4,)),
            dma((band + 4,)),
            dma((2,)),
            dma((2,)),
            dma((4, 2)),
            dma((4, 2)),
            dma((band, lon_size - 1)),
            dma((band, lon_size)),
        ],
        compiler_params=pltpu.CompilerParams(
            collective_id=0, has_side_effects=True, vmem_limit_bytes=56 * 1024 * 1024
        ),
    )(
        circle,
        grid_state[0],
        stencil_one,
        stencil_two,
        norm_gain[None],
        query_weight,
        key_value_weight,
    )
    return (mixed_field[None], attended[None])


def solution(mesh):
    in_specs = (P(None, "lat", "lon", None), P(), P(), P(), P(), P())
    out_specs = (P(None, "lat", "lon", None), P(None, "lat", "lon", None))
    return jax.shard_map(local, mesh=mesh, in_specs=in_specs, out_specs=out_specs, check_vma=False)
```

time: 180 us -> 114 us (0.63)
  the two profiles are of different devices: /device:TPU:25 before, /device:TPU:8 now
where the time goes in v2:
time: 114 us; the launch traced here: 113 us
  Pallas kernels  105 us (92%)
  local copies, waits for them, and re-layouts  7.28 us (6%)
    pallas_call x1, Pallas kernels, local(): pl.pallas_call(functools.partial(block_kernel, lat_size, lon_size), out_s...  105 us
    unnamed x6, local copies, waits for them, and re-layouts  7.28 us

profile of v2, /device:TPU:8, one launch (start us, length us, event | category | flops | bytes accessed | tf_op | source)
XLA Modules:
  0.0 113.4 jit_solution(1011274010075341123)
XLA Ops:
  0.6 0.6 sine_abs_fusion.circle_ref
  1.3 1.4 %copy.8.stencil_one_ref = f32[2,3,1024]{2,1,0:T(4,128)} copy(f32[2,3,1024]{2,0,1:T(2,128)} %param.7) | data formatting | bytes 49152 | tf_op args[1]
  2.6 1.4 %copy.9.stencil_two_ref = f32[2,3,1024]{2,1,0:T(4,128)} copy(f32[2,3,1024]{2,0,1:T(2,128)} %param.8) | data formatting | bytes 49152 | tf_op args[2]
  4.0 104.8 %shard_map.77 = (bf16[4,256,1024]{2,1,0:T(8,128)(2,1)}, bf16[4,256,1024]{2,1,0:T(8,128)(2,1)}) custom-call(f32[8]{0:T(128)} %sine_abs_fusion.circle_ref, bf16[4,256,1024]{2,1,0:T(8,128)(2,1)} %bitcast.4, f32[2,3,1024]{2,1,0:T(4,128)} %copy.8.stencil_one_ref, f32[2,3,1024]{2,1,0:T(4,128)} %copy.9.stencil_two_ref, f32[1,1024]{1,0:T(1,128)} %bitcast.7, ...), custom_call_target="tpu_custom_call" | custom-call | tf_op jit(solution)/shard_map/pallas_call | solution.py:359
  108.8 0.0 copy-start
  108.8 3.2 %copy.12 = bf16[1,4,256,1024]{3,2,1,0:T(8,128)(2,1)} copy(bf16[1,4,256,1024]{3,2,1,0:T(8,128)(2,1)} %bitcast.6) | data formatting | bytes 4194304
  112.0 0.0 copy-done
  112.0 1.3 %copy.13 = bf16[1,4,256,1024]{3,2,1,0:T(8,128)(2,1)} copy(bf16[1,4,256,1024]{3,2,1,0:T(8,128)(2,1)S(1)} %bitcast.5) | data formatting | bytes 4194304
Async XLA Ops:
  108.8 3.2 %copy-start = (bf16[4,256,1024]{2,1,0:T(8,128)(2,1)S(1)}, bf16[4,256,1024]{2,1,0:T(8,128)(2,1)}, u32[]{:S(2)}) copy-start(bf16[4,256,1024]{2,1,0:T(8,128)(2,1)} %get-tuple-element.5) | copy-start | bytes 6291460

commit v3 on v2

v3 whole, which is shorter than its diff:
```python
import functools
import math

import jax
import jax.numpy as jnp
from jax import lax
from jax.experimental import pallas as pl
from jax.experimental.pallas import tpu as pltpu
from jax.sharding import PartitionSpec as P

HEADS = 16
KV_HEADS = 4
HEAD_DIM = 64
GROUPS = HEADS // KV_HEADS
BLOCK = KV_HEADS * HEAD_DIM
EDGE = 16
STENCIL_ONE_ROW, STENCIL_TWO_ROW, GAIN_ROW, CIRCLE_ROW = 0, 6, 12, 13
MESH = pl.DeviceIdType.MESH
QUERY_SCALE = math.log2(math.e) / math.sqrt(HEAD_DIM)


def lane_group(shape):
    return lax.broadcasted_iota(jnp.int32, shape, len(shape) - 1) // HEAD_DIM


def place_queries(normed, query_weight_ref, placed_ref):
    for g in range(KV_HEADS):
        weight = query_weight_ref[:, g * BLOCK : (g + 1) * BLOCK]
        block = jnp.dot(normed, weight, preferred_element_type=jnp.float32) * QUERY_SCALE
        group = lane_group(block.shape)
        for j in range(GROUPS):
            shift = (g - j) * HEAD_DIM % BLOCK
            moved = pltpu.roll(block, shift, 1) if shift else block
            placed_ref[j, g] = jnp.where(group == g, moved, 0.0).astype(jnp.bfloat16)


def attend(placed_ref, keys_ref, values_ref, mixed_ref, store):
    owners = range(keys_ref.shape[0])
    heads = [(j, g) for j in range(GROUPS) for g in range(KV_HEADS)]

    def scores_of(head):
        query = placed_ref[head]
        return [
            jnp.dot(query, keys_ref[o], preferred_element_type=jnp.float32) for o in owners
        ]

    scores = scores_of(heads[0])
    for index, (j, g) in enumerate(heads):
        following = scores_of(heads[index + 1]) if index + 1 < len(heads) else None
        peak = jnp.max(functools.reduce(jnp.maximum, scores), axis=-1, keepdims=True)
        probs = [jnp.exp2(part - peak) for part in scores]
        denominator = jnp.sum(sum(probs[1:], probs[0]), axis=-1, keepdims=True)
        updates = [
            jnp.dot(probs[o].astype(jnp.bfloat16), values_ref[o], preferred_element_type=jnp.float32)
            for o in owners
        ]
        update = sum(updates[1:], updates[0]) / denominator
        if g == 0:
            mixed = update
        else:
            mixed = jnp.where(lane_group(update.shape) == g, update, mixed)
        if g == KV_HEADS - 1:
            mixed_ref[j] = mixed
        scores = following
    for g in range(KV_HEADS):
        out = jnp.zeros(mixed_ref.shape[1:], jnp.float32)
        group = lane_group(out.shape)
        for j in range(GROUPS):
            shift = (j - g) * HEAD_DIM % BLOCK
            part = mixed_ref[j]
            moved = pltpu.roll(part, shift, 1) if shift else part
            out = jnp.where(group == j, moved, out)
        store(g, out.astype(jnp.bfloat16))


def row_weights(first_row, row_count, nlat_total):
    positions = (jnp.arange(row_count, dtype=jnp.int32) + first_row).astype(jnp.float32)
    return jnp.abs(jnp.sin(jnp.pi * (positions + 0.5) / nlat_total))


def block_kernel(
    lat_size,
    lon_size,
    table_ref,
    grid_ref,
    query_hbm,
    key_value_hbm,
    mixed_out,
    attended_out,
    wide,
    after_one,
    mixed_field,
    normed,
    keys,
    values,
    placed,
    mixed,
    attended,
    query_weight,
    key_value_weight,
    local_sem,
    out_sem,
    halo_send,
    halo_recv,
    side_send,
    side_recv,
    edge_send,
    edge_recv,
    kv_send,
    kv_recv,
):
    band, width, channels = grid_ref.shape
    last = band - 1
    lat = lax.axis_index("lat")
    lon = lax.axis_index("lon")
    chips = lon_size // 2
    left, right = lax.rem(lon + lon_size - 1, lon_size), lax.rem(lon + 1, lon_size)
    sibling = lon + 1 - 2 * lax.rem(lon, 2)
    partner = lax.rem(lon + lon_size // 2, lon_size)
    top = (jnp.where(lat == 0, lat, lat - 1), jnp.where(lat == 0, partner, lon))
    at_end = lat == lat_size - 1
    bottom = (jnp.where(at_end, lat, lat + 1), jnp.where(at_end, partner, lon))

    def remote(src, dst, send, recv, device):
        return pltpu.make_async_remote_copy(
            src_ref=src,
            dst_ref=dst,
            send_sem=send,
            recv_sem=recv,
            device_id=device,
            device_id_type=MESH,
        )

    loads = [
        pltpu.make_async_copy(
            grid_ref, wide.at[pl.ds(2, band), pl.ds(EDGE, width)], local_sem.at[0]
        ),
        pltpu.make_async_copy(key_value_hbm, key_value_weight, local_sem.at[1]),
        pltpu.make_async_copy(query_hbm, query_weight, local_sem.at[2]),
    ]
    for load in loads:
        load.start()

    barrier = pltpu.get_barrier_semaphore()
    for device in (top, bottom):
        pl.semaphore_signal(barrier, inc=1, device_id=device, device_id_type=MESH)
    for step in range(1, lon_size):
        other = (lat, lax.rem(lon + step, lon_size))
        pl.semaphore_signal(barrier, inc=1, device_id=other, device_id_type=MESH)
    pl.semaphore_wait(barrier, lon_size + 1)

    def from_top(stage):
        return lax.rem(lat + stage, 2) == 1

    def halo_row(stage):
        far = stage // 2
        return jnp.where(from_top(stage), 1 - far, band + 2 + far)

    def mixed_row(stage):
        near = 1 - stage // 2
        return jnp.where(from_top(stage), near, last - near)

    def halo_copy(stage):
        far = stage // 2
        up = from_top(stage)
        pole = lat == jnp.where(up, 0, lat_size - 1)
        source = jnp.where(up, far, last - far)
        target = jnp.where(up == pole, 1 - far, band + 2 + far)
        device = (
            jnp.where(pole, lat, jnp.where(up, lat - 1, lat + 1)),
            jnp.where(pole, partner, lon),
        )
        return remote(
            grid_ref.at[source],
            wide.at[target, pl.ds(EDGE, width)],
            halo_send.at[stage],
            halo_recv.at[stage],
            device,
        )

    def halo_arrival(stage):
        block = wide.at[halo_row(stage), pl.ds(EDGE, width)]
        return remote(block, block, halo_send.at[stage], halo_recv.at[stage], (lat, sibling))

    sides = [
        remote(
            grid_ref.at[:, pl.ds(width - EDGE, EDGE)],
            wide.at[pl.ds(2, band), pl.ds(0, EDGE)],
            side_send.at[0],
            side_recv.at[0],
            (lat, right),
        ),
        remote(
            grid_ref.at[:, pl.ds(0, EDGE)],
            wide.at[pl.ds(2, band), pl.ds(EDGE + width, EDGE)],
            side_send.at[1],
            side_recv.at[1],
            (lat, left),
        ),
    ]
    for side in sides:
        side.start()
    halo_copy(0).start()

    def edges(stage):
        row = halo_row(stage)
        return [
            remote(
                wide.at[row, pl.ds(width, EDGE)],
                wide.at[row, pl.ds(0, EDGE)],
                edge_send.at[stage, 0],
                edge_recv.at[stage, 0],
                (lat, right),
            ),
            remote(
                wide.at[row, pl.ds(EDGE, EDGE)],
                wide.at[row, pl.ds(EDGE + width, EDGE)],
                edge_send.at[stage, 1],
                edge_recv.at[stage, 1],
                (lat, left),
            ),
        ]

    def stencil(source, first, count, circle_first, weights_first, store):
        total = width + 2 * EDGE
        chunks = channels // 128

        def one(index, carry):
            row = first + index // chunks
            circle = CIRCLE_ROW + circle_first + index // chunks
            lanes = pl.ds(pl.multiple_of(index % chunks * 128, 128), 128)
            above = source[row - 1, :, lanes].astype(jnp.float32)
            centre = source[row, :, lanes].astype(jnp.float32)
            below = source[row + 1, :, lanes].astype(jnp.float32)
            above_factor = table_ref[circle - 1, :, lanes]
            own_factor = table_ref[circle, :, lanes]
            below_factor = table_ref[circle + 1, :, lanes]
            beside = above_factor * above + below_factor * below
            taps = []
            for offset in range(3):
                own = table_ref[weights_first + offset, :, lanes] * own_factor
                next_to = table_ref[weights_first + 3 + offset, :, lanes]
                taps.append(own * centre + next_to * beside)
            result = centre + taps[1] + pltpu.roll(taps[0], 1, 0)
            result = result + pltpu.roll(taps[2], total - 1, 0)
            store(row, lanes, result.astype(jnp.bfloat16))
            return carry

        lax.fori_loop(0, count * chunks, one, 0)

    def store_after_one(row, lanes, value):
        after_one[row - 1, :, lanes] = value

    def store_mixed(row, lanes, value):
        mixed_field[row - 1, :, lanes] = value[EDGE : EDGE + width]

    def kv_copies(row, owner, device, slot):
        return [
            remote(
                held.at[row, owner],
                held.at[row, owner],
                kv_send.at[kind, row, slot],
                kv_recv.at[kind, row, owner],
                device,
            )
            for kind, held in enumerate((keys, values))
        ]

    def kv_start(row):
        for step in range(1, chips):
            for copy in kv_copies(row, lon, (lat, lax.rem(lon + 2 * step, lon_size)), step):
                copy.start()
        for copy in kv_copies(row, lon, (lat, sibling), 0):
            copy.start()

    def kv_forward(row):
        for step in range(1, chips):
            owner = lax.rem(lon + lon_size - 2 * step, lon_size)
            for copy in kv_copies(row, owner, (lat, sibling), chips - 1 + step):
                copy.wait_recv()
                copy.start()

    def kv_collect(row):
        for step in range(chips):
            owner = lax.rem(sibling + lon_size - 2 * step, lon_size)
            for copy in kv_copies(row, owner, (lat, sibling), 0):
                copy.wait_recv()

    def mixed_copy(row):
        return pltpu.make_async_copy(mixed_field.at[row], mixed_out.at[row], out_sem.at[0, row])

    def attended_copy(row):
        return pltpu.make_async_copy(attended.at[row], attended_out.at[row], out_sem.at[1, row])

    def project(row):
        tokens = mixed_field[row].astype(jnp.float32)
        mean_square = jnp.mean(tokens * tokens, axis=-1, keepdims=True)
        scaled = tokens * lax.rsqrt(mean_square + 1e-06) * table_ref[GAIN_ROW]
        normed[row] = scaled.astype(jnp.bfloat16)
        both = jnp.dot(normed[row], key_value_weight[...], preferred_element_type=jnp.float32)
        keys[row, lon] = jnp.transpose(both[:, :BLOCK]).astype(jnp.bfloat16)
        values[row, lon] = both[:, BLOCK:].astype(jnp.bfloat16)
        kv_start(row)
        mixed_copy(row).start()

    def attend_row(row):
        kv_forward(row)
        place_queries(normed[row], query_weight, placed)
        kv_collect(row)

        def store(g, value):
            attended[row, :, g * BLOCK : (g + 1) * BLOCK] = value

        attend(placed, keys.at[row], values.at[row], mixed, store)
        attended_copy(row).start()

    loads[0].wait()
    for side in sides:
        side.wait_recv()
    stencil(wide, 3, band - 2, 3, STENCIL_ONE_ROW, store_after_one)
    loads[1].wait()
    loads[2].wait()

    def one_stage(stage, carry):
        @pl.when(stage < band)
        def _():
            halo_copy(stage).wait_send()

            @pl.when(stage < band - 1)
            def _():
                halo_copy(stage + 1).start()

            halo_arrival(stage).wait_recv()
            for edge in edges(stage):
                edge.start()
            for edge in edges(stage):
                edge.wait_recv()
            row = mixed_row(stage)
            outer = jnp.where(from_top(stage), row + 1, row + 3)
            stencil(wide, outer, 1, outer, STENCIL_ONE_ROW, store_after_one)
            stencil(after_one, row + 1, 1, row + 2, STENCIL_TWO_ROW, store_mixed)
            project(row)

        @pl.when(stage > 0)
        def _():
            attend_row(mixed_row(stage - 1))

        return carry

    lax.fori_loop(0, band + 1, one_stage, 0)

    for side in sides:
        side.wait_send()

    def finish(row, carry):
        for edge in edges(row):
            edge.wait_send()
        for slot in range(lon_size - 1):
            for copy in kv_copies(row, lon, (lat, sibling), slot):
                copy.wait_send()
        mixed_copy(row).wait()
        attended_copy(row).wait()
        return carry

    lax.fori_loop(0, band, finish, 0)


def local(grid_state, stencil_one, stencil_two, norm_gain, query_weight, key_value_weight):
    level_count, band, width, channels = grid_state.shape
    lat_size, lon_size = lax.axis_size("lat"), lax.axis_size("lon")
    circle = row_weights(lax.axis_index("lat") * band - 2, band + 4, band * lat_size)
    table = jnp.concatenate(
        [
            stencil_one.reshape(6, channels),
            stencil_two.reshape(6, channels),
            norm_gain[None],
            jnp.broadcast_to(circle[:, None], (band + 4, channels)),
        ]
    )[:, None]
    whole = pl.BlockSpec(memory_space=pltpu.VMEM)
    anywhere = pl.BlockSpec(memory_space=pl.ANY)
    field = jax.ShapeDtypeStruct((band, width, channels), jnp.bfloat16)
    wide_width = width + 2 * EDGE
    rows = (band, width, channels)
    dma = pltpu.SemaphoreType.DMA
    mixed_field, attended = pl.pallas_call(
        functools.partial(block_kernel, lat_size, lon_size),
        out_shape=(field, field),
        in_specs=[
            whole,
            anywhere,
            anywhere,
            anywhere,
        ],
        out_specs=(anywhere, anywhere),
        scratch_shapes=[
            pltpu.VMEM((band + 4, wide_width, channels), jnp.bfloat16),
            pltpu.VMEM((band + 2, wide_width, channels), jnp.bfloat16),
            pltpu.VMEM(rows, jnp.bfloat16),
            pltpu.VMEM(rows, jnp.bfloat16),
            pltpu.VMEM((band, lon_size, BLOCK, width), jnp.bfloat16),
            pltpu.VMEM((band, lon_size, width, BLOCK), jnp.bfloat16),
            pltpu.VMEM((GROUPS, KV_HEADS, width, BLOCK), jnp.bfloat16),
            pltpu.VMEM((GROUPS, width, BLOCK), jnp.float32),
            pltpu.VMEM(rows, jnp.bfloat16),
            pltpu.VMEM(query_weight.shape, jnp.bfloat16),
            pltpu.VMEM(key_value_weight.shape, jnp.bfloat16),
            dma((3,)),
            dma((2, band)),
            dma((4,)),
            dma((4,)),
            dma((2,)),
            dma((2,)),
            dma((4, 2)),
            dma((4, 2)),
            dma((2, band, lon_size - 1)),
            dma((2, band, lon_size)),
        ],
        compiler_params=pltpu.CompilerParams(
            collective_id=0, has_side_effects=True, vmem_limit_bytes=56 * 1024 * 1024
        ),
    )(
        table,
        grid_state[0],
        query_weight,
        key_value_weight,
    )
    return (mixed_field[None], attended[None])


def solution(mesh):
    in_specs = (P(None, "lat", "lon", None), P(), P(), P(), P(), P())
    out_specs = (P(None, "lat", "lon", None), P(None, "lat", "lon", None))
    return jax.shard_map(local, mesh=mesh, in_specs=in_specs, out_specs=out_specs, check_vma=False)
```

time: 114 us -> 104 us (0.912)
  the two profiles are of different devices: /device:TPU:8 before, /device:TPU:0 now
where the time goes in v3:
time: 104 us
  Pallas kernels  95.8 us (92%)
  local copies, waits for them, and re-layouts  6.87 us (7%)
    pallas_call x1, Pallas kernels, local(): pl.pallas_call(functools.partial(block_kernel, lat_size, lon_size), out_s...  95.8 us
    unnamed x6, local copies, waits for them, and re-layouts  6.06 us

profile of v3, /device:TPU:0, one launch (start us, length us, event | category | flops | bytes accessed | tf_op | source)
XLA Modules:
  0.0 104.2 jit_solution(16371541636545704475)
XLA Ops:
  0.7 0.1 pad.3.clone
  0.8 0.8 copy.10
  1.5 0.8 copy.11
  2.3 0.8 maximum_maximum_fusion
  3.1 0.7 broadcast_in_dim.20.table_ref
  3.8 95.8 %shard_map.77 = (bf16[4,256,1024]{2,1,0:T(8,128)(2,1)}, bf16[4,256,1024]{2,1,0:T(8,128)(2,1)}) custom-call(f32[21,1,1024]{2,1,0:T(1,128)} %broadcast_in_dim.20.table_ref, bf16[4,256,1024]{2,1,0:T(8,128)(2,1)} %bitcast.4, bf16[1024,1024]{1,0:T(8,128)(2,1)} %query_hbm.1, bf16[1024,512]{1,0:T(8,128)(2,1)} %key_value_hbm.1), custom_call_target="tpu_custom_call" | custom-call | tf_op jit(solution)/shard_map/pallas_call | solution.py:386
  99.6 0.0 copy-start
  99.6 3.2 %copy.14 = bf16[1,4,256,1024]{3,2,1,0:T(8,128)(2,1)} copy(bf16[1,4,256,1024]{3,2,1,0:T(8,128)(2,1)} %bitcast.6) | data formatting | bytes 4194304
  102.9 0.0 copy-done
  102.9 1.3 %copy.15 = bf16[1,4,256,1024]{3,2,1,0:T(8,128)(2,1)} copy(bf16[1,4,256,1024]{3,2,1,0:T(8,128)(2,1)S(1)} %bitcast.5) | data formatting | bytes 4194304
  (3 shorter events, 0.1 us)
Async XLA Ops:
  99.6 3.2 %copy-start = (bf16[4,256,1024]{2,1,0:T(8,128)(2,1)S(1)}, bf16[4,256,1024]{2,1,0:T(8,128)(2,1)}, u32[]{:S(2)}) copy-start(bf16[4,256,1024]{2,1,0:T(8,128)(2,1)} %get-tuple-element.5) | copy-start | bytes 6291460

commit v4 on v3

--- a/solution.py
+++ b/solution.py
@@ -14,7 +14,7 @@
 GROUPS = HEADS // KV_HEADS
 BLOCK = KV_HEADS * HEAD_DIM
 EDGE = 16
-STENCIL_ONE_ROW, STENCIL_TWO_ROW, GAIN_ROW, CIRCLE_ROW = 0, 6, 12, 13
+STENCIL_ONE_ROW, STENCIL_TWO_ROW, GAIN_ROW = 0, 6, 12
 MESH = pl.DeviceIdType.MESH
 QUERY_SCALE = math.log2(math.e) / math.sqrt(HEAD_DIM)
 
@@ -36,6 +36,7 @@
 
 def attend(placed_ref, keys_ref, values_ref, mixed_ref, store):
     owners = range(keys_ref.shape[0])
+    columns = keys_ref.shape[0] * keys_ref.shape[2]
     heads = [(j, g) for j in range(GROUPS) for g in range(KV_HEADS)]
 
     def scores_of(head):
@@ -50,11 +51,10 @@
         peak = jnp.max(functools.reduce(jnp.maximum, scores), axis=-1, keepdims=True)
         probs = [jnp.exp2(part - peak) for part in scores]
         denominator = jnp.sum(sum(probs[1:], probs[0]), axis=-1, keepdims=True)
-        updates = [
-            jnp.dot(probs[o].astype(jnp.bfloat16), values_ref[o], preferred_element_type=jnp.float32)
-            for o in owners
-        ]
-        update = sum(updates[1:], updates[0]) / denominator
+        rounded = jnp.concatenate([part.astype(jnp.bfloat16) for part in probs], axis=1)
+        update = jnp.dot(
+            rounded, values_ref[...].reshape(columns, BLOCK), preferred_element_type=jnp.float32
+        ) * (1.0 / denominator)
         if g == 0:
             mixed = update
         else:
@@ -71,11 +71,6 @@
             moved = pltpu.roll(part, shift, 1) if shift else part
             out = jnp.where(group == j, moved, out)
         store(g, out.astype(jnp.bfloat16))
-
-
-def row_weights(first_row, row_count, nlat_total):
-    positions = (jnp.arange(row_count, dtype=jnp.int32) + first_row).astype(jnp.float32)
-    return jnp.abs(jnp.sin(jnp.pi * (positions + 0.5) / nlat_total))
 
 
 def block_kernel(
@@ -98,6 +93,7 @@
     attended,
     query_weight,
     key_value_weight,
+    circle_ref,
     local_sem,
     out_sem,
     halo_send,
@@ -202,6 +198,12 @@
         side.start()
     halo_copy(0).start()
 
+    at_pole = jnp.logical_or(lat == 0, at_end)
+
+    @pl.when(at_pole)
+    def _():
+        halo_copy(1).start()
+
     def edges(stage):
         row = halo_row(stage)
         return [
@@ -221,38 +223,49 @@
             ),
         ]
 
-    def stencil(source, first, count, circle_first, weights_first, store):
-        total = width + 2 * EDGE
+    def stencil(source, first, count, circle_first, weights_first, store, strips):
         chunks = channels // 128
 
         def one(index, carry):
             row = first + index // chunks
-            circle = CIRCLE_ROW + circle_first + index // chunks
+            circle = circle_first + index // chunks
             lanes = pl.ds(pl.multiple_of(index % chunks * 128, 128), 128)
-            above = source[row - 1, :, lanes].astype(jnp.float32)
-            centre = source[row, :, lanes].astype(jnp.float32)
-            below = source[row + 1, :, lanes].astype(jnp.float32)
-            above_factor = table_ref[circle - 1, :, lanes]
-            own_factor = table_ref[circle, :, lanes]
-            below_factor = table_ref[circle + 1, :, lanes]
-            beside = above_factor * above + below_factor * below
-            taps = []
-            for offset in range(3):
-                own = table_ref[weights_first + offset, :, lanes] * own_factor
-                next_to = table_ref[weights_first + 3 + offset, :, lanes]
-                taps.append(own * centre + next_to * beside)
-            result = centre + taps[1] + pltpu.roll(taps[0], 1, 0)
-            result = result + pltpu.roll(taps[2], total - 1, 0)
-            store(row, lanes, result.astype(jnp.bfloat16))
+            factors = [circle_ref[circle + offset] for offset in (-1, 0, 1)]
+            own = [
+                table_ref[weights_first + offset, :, lanes] * factors[1] for offset in range(3)
+            ]
+            next_to = [table_ref[weights_first + 3 + offset, :, lanes] for offset in range(3)]
+
+            def taps(strip):
+                columns = pl.ds(strip * EDGE, EDGE)
+                above = source[row - 1, columns, lanes].astype(jnp.float32)
+                centre = source[row, columns, lanes].astype(jnp.float32)
+                below = source[row + 1, columns, lanes].astype(jnp.float32)
+                beside = factors[0] * above + factors[2] * below
+                parts = [own[offset] * centre + next_to[offset] * beside for offset in range(3)]
+                return parts[0], centre + parts[1], parts[2]
+
+            start, stop = strips
+            before, here = taps(max(start - 1, 0)), taps(start)
+            for strip in range(start, stop):
+                after = taps(min(strip + 1, width // EDGE + 1))
+                west = jnp.concatenate([before[0][8:], here[0]], axis=0)
+                east = jnp.concatenate([here[2], after[2][:8]], axis=0)
+                result = here[1] + pltpu.roll(west, 1, 0)[8:] + pltpu.roll(east, 23, 0)[:EDGE]
+                store(row, strip, lanes, result.astype(jnp.bfloat16))
+                before, here = here, after
             return carry
 
         lax.fori_loop(0, count * chunks, one, 0)
 
-    def store_after_one(row, lanes, value):
-        after_one[row - 1, :, lanes] = value
-
-    def store_mixed(row, lanes, value):
-        mixed_field[row - 1, :, lanes] = value[EDGE : EDGE + width]
+    inner = (1, width // EDGE + 1)
+    outward = (0, width // EDGE + 2)
+
+    def store_after_one(row, strip, lanes, value):
+        after_one[row - 1, pl.ds(strip * EDGE, EDGE), lanes] = value
+
+    def store_mixed(row, strip, lanes, value):
+        mixed_field[row - 1, pl.ds((strip - 1) * EDGE, EDGE), lanes] = value
 
     def kv_copies(row, owner, device, slot):
         return [
@@ -314,21 +327,43 @@
         attend(placed, keys.at[row], values.at[row], mixed, store)
         attended_copy(row).start()
 
+    positions = lax.broadcasted_iota(jnp.int32, circle_ref.shape, 0) + (lat * band - 2)
+    angle = jnp.pi * (positions.astype(jnp.float32) + 0.5) / (band * lat_size)
+    circle_ref[...] = jnp.abs(jnp.sin(angle))
+
     loads[0].wait()
     for side in sides:
         side.wait_recv()
-    stencil(wide, 3, band - 2, 3, STENCIL_ONE_ROW, store_after_one)
+    stencil(wide, 3, band - 2, 3, STENCIL_ONE_ROW, store_after_one, outward)
     loads[1].wait()
     loads[2].wait()
 
     def one_stage(stage, carry):
         @pl.when(stage < band)
         def _():
-            halo_copy(stage).wait_send()
-
-            @pl.when(stage < band - 1)
+            @pl.when(at_pole)
             def _():
-                halo_copy(stage + 1).start()
+                @pl.when(stage == 0)
+                def _():
+                    halo_copy(0).wait_send()
+                    halo_copy(1).wait_send()
+                    halo_copy(3).start()
+
+                @pl.when(stage == 1)
+                def _():
+                    halo_copy(2).start()
+
+                @pl.when(stage > 1)
+                def _():
+                    halo_copy(stage).wait_send()
+
+            @pl.when(jnp.logical_not(at_pole))
+            def _():
+                halo_copy(stage).wait_send()
+
+                @pl.when(stage < band - 1)
+                def _():
+                    halo_copy(stage + 1).start()
 
             halo_arrival(stage).wait_recv()
             for edge in edges(stage):
@@ -337,8 +372,8 @@
                 edge.wait_recv()
             row = mixed_row(stage)
             outer = jnp.where(from_top(stage), row + 1, row + 3)
-            stencil(wide, outer, 1, outer, STENCIL_ONE_ROW, store_after_one)
-            stencil(after_one, row + 1, 1, row + 2, STENCIL_TWO_ROW, store_mixed)
+            stencil(wide, outer, 1, outer, STENCIL_ONE_ROW, store_after_one, outward)
+            stencil(after_one, row + 1, 1, row + 2, STENCIL_TWO_ROW, store_mixed, inner)
             project(row)
 
         @pl.when(stage > 0)
@@ -368,14 +403,10 @@
 def local(grid_state, stencil_one, stencil_two, norm_gain, query_weight, key_value_weight):
     level_count, band, width, channels = grid_state.shape
     lat_size, lon_size = lax.axis_size("lat"), lax.axis_size("lon")
-    circle = row_weights(lax.axis_index("lat") * band - 2, band + 4, band * lat_size)
-    table = jnp.concatenate(
-        [
-            stencil_one.reshape(6, channels),
-            stencil_two.reshape(6, channels),
-            norm_gain[None],
-            jnp.broadcast_to(circle[:, None], (band + 4, channels)),
-        ]
+    table = jnp.stack(
+        [stencil_one[a, b] for a in range(2) for b in range(3)]
+        + [stencil_two[a, b] for a in range(2) for b in range(3)]
+        + [norm_gain]
     )[:, None]
     whole = pl.BlockSpec(memory_space=pltpu.VMEM)
     anywhere = pl.BlockSpec(memory_space=pl.ANY)
@@ -405,6 +436,7 @@
             pltpu.VMEM(rows, jnp.bfloat16),
             pltpu.VMEM(query_weight.shape, jnp.bfloat16),
             pltpu.VMEM(key_value_weight.shape, jnp.bfloat16),
+            pltpu.VMEM((band + 4, 1, 128), jnp.float32),
             dma((3,)),
             dma((2, band)),
             dma((4,)),

time: 104 us -> 99.8 us (0.960)
  the two profiles are of different devices: /device:TPU:0 before, /device:TPU:25 now
where the time goes in v4:
time: 99.8 us; the launch traced here: 99.5 us
  Pallas kernels  92 us (92%)
  local copies, waits for them, and re-layouts  6.89 us (7%)
    pallas_call x1, Pallas kernels, local(): pl.pallas_call(functools.partial(block_kernel, lat_size, lon_size), out_s...  92 us
    unnamed x4, local copies, waits for them, and re-layouts  4.55 us

profile of v4, /device:TPU:25, one launch (start us, length us, event | category | flops | bytes accessed | tf_op | source)
XLA Modules:
  0.0 99.5 jit_solution(2323307891514035451)
XLA Ops:
  0.6 0.9 slice_bitcast_fusion
  1.5 0.8 stack.7
  2.3 0.7 broadcast_in_dim.9.table_ref
  3.0 92.0 %shard_map.77 = (bf16[4,256,1024]{2,1,0:T(8,128)(2,1)}, bf16[4,256,1024]{2,1,0:T(8,128)(2,1)}) custom-call(f32[13,1,1024]{2,1,0:T(1,128)} %broadcast_in_dim.9.table_ref, bf16[4,256,1024]{2,1,0:T(8,128)(2,1)} %bitcast.28, bf16[1024,1024]{1,0:T(8,128)(2,1)} %query_hbm.1, bf16[1024,512]{1,0:T(8,128)(2,1)} %key_value_hbm.1), custom_call_target="tpu_custom_call" | custom-call | tf_op jit(solution)/shard_map/pallas_call | solution.py:417
  95.0 0.0 copy-start
  95.0 3.2 %copy.10 = bf16[1,4,256,1024]{3,2,1,0:T(8,128)(2,1)} copy(bf16[1,4,256,1024]{3,2,1,0:T(8,128)(2,1)} %bitcast.30) | data formatting | bytes 4194304
  98.2 0.0 copy-done
  98.2 1.3 %copy.11 = bf16[1,4,256,1024]{3,2,1,0:T(8,128)(2,1)} copy(bf16[1,4,256,1024]{3,2,1,0:T(8,128)(2,1)S(1)} %bitcast.29) | data formatting | bytes 4194304
Async XLA Ops:
  95.0 3.2 %copy-start = (bf16[4,256,1024]{2,1,0:T(8,128)(2,1)S(1)}, bf16[4,256,1024]{2,1,0:T(8,128)(2,1)}, u32[]{:S(2)}) copy-start(bf16[4,256,1024]{2,1,0:T(8,128)(2,1)} %get-tuple-element.5) | copy-start | bytes 6291460

commit v5 on v4

--- a/solution.py
+++ b/solution.py
@@ -17,6 +17,7 @@
 STENCIL_ONE_ROW, STENCIL_TWO_ROW, GAIN_ROW = 0, 6, 12
 MESH = pl.DeviceIdType.MESH
 QUERY_SCALE = math.log2(math.e) / math.sqrt(HEAD_DIM)
+BUNDLE = 2
 
 
 def lane_group(shape):
@@ -37,17 +38,19 @@
 def attend(placed_ref, keys_ref, values_ref, mixed_ref, store):
     owners = range(keys_ref.shape[0])
     columns = keys_ref.shape[0] * keys_ref.shape[2]
-    heads = [(j, g) for j in range(GROUPS) for g in range(KV_HEADS)]
-
-    def scores_of(head):
-        query = placed_ref[head]
+    width = mixed_ref.shape[1]
+    bundles = [(j, g) for j in range(GROUPS) for g in range(0, KV_HEADS, BUNDLE)]
+
+    def scores_of(bundle):
+        j, g = bundle
+        query = placed_ref[j, g : g + BUNDLE].reshape(BUNDLE * width, BLOCK)
         return [
             jnp.dot(query, keys_ref[o], preferred_element_type=jnp.float32) for o in owners
         ]
 
-    scores = scores_of(heads[0])
-    for index, (j, g) in enumerate(heads):
-        following = scores_of(heads[index + 1]) if index + 1 < len(heads) else None
+    scores = scores_of(bundles[0])
+    for index, (j, first) in enumerate(bundles):
+        following = scores_of(bundles[index + 1]) if index + 1 < len(bundles) else None
         peak = jnp.max(functools.reduce(jnp.maximum, scores), axis=-1, keepdims=True)
         probs = [jnp.exp2(part - peak) for part in scores]
         denominator = jnp.sum(sum(probs[1:], probs[0]), axis=-1, keepdims=True)
@@ -55,11 +58,10 @@
         update = jnp.dot(
             rounded, values_ref[...].reshape(columns, BLOCK), preferred_element_type=jnp.float32
         ) * (1.0 / denominator)
-        if g == 0:
-            mixed = update
-        else:
-            mixed = jnp.where(lane_group(update.shape) == g, update, mixed)
-        if g == KV_HEADS - 1:
+        for g in range(first, first + BUNDLE):
+            part = update[(g - first) * width : (g - first + 1) * width]
+            mixed = part if g == 0 else jnp.where(lane_group(part.shape) == g, part, mixed)
+        if first + BUNDLE == KV_HEADS:
             mixed_ref[j] = mixed
         scores = following
     for g in range(KV_HEADS):

time: 99.8 us -> 99.4 us (level)
  no operation moved by 1% of the time
where the time goes in v5:
time: 99.4 us; the launch traced here: 99.1 us
  Pallas kernels  91.6 us (92%)
  local copies, waits for them, and re-layouts  6.89 us (7%)
    pallas_call x1, Pallas kernels, local(): pl.pallas_call(functools.partial(block_kernel, lat_size, lon_size), out_s...  91.6 us
    unnamed x4, local copies, waits for them, and re-layouts  4.55 us

profile of v5, /device:TPU:25, one launch (start us, length us, event | category | flops | bytes accessed | tf_op | source)
XLA Modules:
  0.0 99.1 jit_solution(17162640991545006184)
XLA Ops:
  0.6 0.9 slice_bitcast_fusion
  1.5 0.8 stack.7
  2.3 0.7 broadcast_in_dim.9.table_ref
  3.0 91.6 %shard_map.77 = (bf16[4,256,1024]{2,1,0:T(8,128)(2,1)}, bf16[4,256,1024]{2,1,0:T(8,128)(2,1)}) custom-call(f32[13,1,1024]{2,1,0:T(1,128)} %broadcast_in_dim.9.table_ref, bf16[4,256,1024]{2,1,0:T(8,128)(2,1)} %bitcast.28, bf16[1024,1024]{1,0:T(8,128)(2,1)} %query_hbm.1, bf16[1024,512]{1,0:T(8,128)(2,1)} %key_value_hbm.1), custom_call_target="tpu_custom_call" | custom-call | tf_op jit(solution)/shard_map/pallas_call | solution.py:419
  94.6 0.0 copy-start
  94.6 3.2 %copy.10 = bf16[1,4,256,1024]{3,2,1,0:T(8,128)(2,1)} copy(bf16[1,4,256,1024]{3,2,1,0:T(8,128)(2,1)} %bitcast.30) | data formatting | bytes 4194304
  97.8 0.0 copy-done
  97.8 1.3 %copy.11 = bf16[1,4,256,1024]{3,2,1,0:T(8,128)(2,1)} copy(bf16[1,4,256,1024]{3,2,1,0:T(8,128)(2,1)S(1)} %bitcast.29) | data formatting | bytes 4194304
Async XLA Ops:
  94.6 3.2 %copy-start = (bf16[4,256,1024]{2,1,0:T(8,128)(2,1)S(1)}, bf16[4,256,1024]{2,1,0:T(8,128)(2,1)}, u32[]{:S(2)}) copy-start(bf16[4,256,1024]{2,1,0:T(8,128)(2,1)} %get-tuple-element.5) | copy-start | bytes 6291460

commit v6 on v5

--- a/solution.py
+++ b/solution.py
@@ -14,7 +14,6 @@
 GROUPS = HEADS // KV_HEADS
 BLOCK = KV_HEADS * HEAD_DIM
 EDGE = 16
-STENCIL_ONE_ROW, STENCIL_TWO_ROW, GAIN_ROW = 0, 6, 12
 MESH = pl.DeviceIdType.MESH
 QUERY_SCALE = math.log2(math.e) / math.sqrt(HEAD_DIM)
 BUNDLE = 2
@@ -78,7 +77,10 @@
 def block_kernel(
     lat_size,
     lon_size,
-    table_ref,
+    *refs,
+):
+    taps_one, taps_two, gain_ref = refs[:6], refs[6:12], refs[12]
+    (
     grid_ref,
     query_hbm,
     key_value_hbm,
@@ -106,7 +108,7 @@
     edge_recv,
     kv_send,
     kv_recv,
-):
+    ) = refs[13:]
     band, width, channels = grid_ref.shape
     last = band - 1
     lat = lax.axis_index("lat")
@@ -225,7 +227,7 @@
             ),
         ]
 
-    def stencil(source, first, count, circle_first, weights_first, store, strips):
+    def stencil(source, first, count, circle_first, weights, store, strips):
         chunks = channels // 128
 
         def one(index, carry):
@@ -233,10 +235,8 @@
             circle = circle_first + index // chunks
             lanes = pl.ds(pl.multiple_of(index % chunks * 128, 128), 128)
             factors = [circle_ref[circle + offset] for offset in (-1, 0, 1)]
-            own = [
-                table_ref[weights_first + offset, :, lanes] * factors[1] for offset in range(3)
-            ]
-            next_to = [table_ref[weights_first + 3 + offset, :, lanes] for offset in range(3)]
+            own = [weights[offset][:, lanes] * factors[1] for offset in range(3)]
+            next_to = [weights[3 + offset][:, lanes] for offset in range(3)]
 
             def taps(strip):
                 columns = pl.ds(strip * EDGE, EDGE)
@@ -310,7 +310,7 @@
     def project(row):
         tokens = mixed_field[row].astype(jnp.float32)
         mean_square = jnp.mean(tokens * tokens, axis=-1, keepdims=True)
-        scaled = tokens * lax.rsqrt(mean_square + 1e-06) * table_ref[GAIN_ROW]
+        scaled = tokens * lax.rsqrt(mean_square + 1e-06) * gain_ref[...]
         normed[row] = scaled.astype(jnp.bfloat16)
         both = jnp.dot(normed[row], key_value_weight[...], preferred_element_type=jnp.float32)
         keys[row, lon] = jnp.transpose(both[:, :BLOCK]).astype(jnp.bfloat16)
@@ -336,13 +336,12 @@
     loads[0].wait()
     for side in sides:
         side.wait_recv()
-    stencil(wide, 3, band - 2, 3, STENCIL_ONE_ROW, store_after_one, outward)
+    stencil(wide, 3, band - 2, 3, taps_one, store_after_one, outward)
     loads[1].wait()
     loads[2].wait()
 
-    def one_stage(stage, carry):
-        @pl.when(stage < band)
-        def _():
+    def one_half(half, carry):
+        def one_stage(stage, carry):
             @pl.when(at_pole)
             def _():
                 @pl.when(stage == 0)
@@ -363,9 +362,14 @@
             def _():
                 halo_copy(stage).wait_send()
 
-                @pl.when(stage < band - 1)
+                @pl.when(stage == 0)
                 def _():
-                    halo_copy(stage + 1).start()
+                    halo_copy(1).start()
+
+                @pl.when(stage == 1)
+                def _():
+                    halo_copy(2).start()
+                    halo_copy(3).start()
 
             halo_arrival(stage).wait_recv()
             for edge in edges(stage):
@@ -374,17 +378,20 @@
                 edge.wait_recv()
             row = mixed_row(stage)
             outer = jnp.where(from_top(stage), row + 1, row + 3)
-            stencil(wide, outer, 1, outer, STENCIL_ONE_ROW, store_after_one, outward)
-            stencil(after_one, row + 1, 1, row + 2, STENCIL_TWO_ROW, store_mixed, inner)
+            stencil(wide, outer, 1, outer, taps_one, store_after_one, outward)
+            stencil(after_one, row + 1, 1, row + 2, taps_two, store_mixed, inner)
             project(row)
-
-        @pl.when(stage > 0)
-        def _():
-            attend_row(mixed_row(stage - 1))
-
+            return carry
+
+        def one_row(stage, carry):
+            attend_row(mixed_row(stage))
+            return carry
+
+        lax.fori_loop(2 * half, 2 * half + 2, one_stage, 0)
+        lax.fori_loop(2 * half, 2 * half + 2, one_row, 0)
         return carry
 
-    lax.fori_loop(0, band + 1, one_stage, 0)
+    lax.fori_loop(0, band // 2, one_half, 0)
 
     for side in sides:
         side.wait_send()
@@ -405,11 +412,12 @@
 def local(grid_state, stencil_one, stencil_two, norm_gain, query_weight, key_value_weight):
     level_count, band, width, channels = grid_state.shape
     lat_size, lon_size = lax.axis_size("lat"), lax.axis_size("lon")
-    table = jnp.stack(
-        [stencil_one[a, b] for a in range(2) for b in range(3)]
-        + [stencil_two[a, b] for a in range(2) for b in range(3)]
-        + [norm_gain]
-    )[:, None]
+    taps = [
+        weights[beside, offset][None]
+        for weights in (stencil_one, stencil_two)
+        for beside in range(2)
+        for offset in range(3)
+    ]
     whole = pl.BlockSpec(memory_space=pltpu.VMEM)
     anywhere = pl.BlockSpec(memory_space=pl.ANY)
     field = jax.ShapeDtypeStruct((band, width, channels), jnp.bfloat16)
@@ -420,7 +428,7 @@
         functools.partial(block_kernel, lat_size, lon_size),
         out_shape=(field, field),
         in_specs=[
-            whole,
+            *[whole] * 13,
             anywhere,
             anywhere,
             anywhere,
@@ -454,7 +462,8 @@
             collective_id=0, has_side_effects=True, vmem_limit_bytes=56 * 1024 * 1024
         ),
     )(
-        table,
+        *taps,
+        norm_gain[None],
         grid_state[0],
         query_weight,
         key_value_weight,

time: 99.4 us -> 106 us (1.066)
  the two profiles are of different devices: /device:TPU:25 before, /device:TPU:17 now
where the time goes in v6:
time: 106 us
  Pallas kernels  99.2 us (94%)
  local copies, waits for them, and re-layouts  6.04 us (6%)
    pallas_call x1, Pallas kernels, local(): pl.pallas_call(functools.partial(block_kernel, lat_size, lon_size), out_s...  99.2 us
    unnamed x4, local copies, waits for them, and re-layouts  4.55 us

profile of v6, /device:TPU:17, one launch (start us, length us, event | category | flops | bytes accessed | tf_op | source)
XLA Modules:
  0.0 105.9 jit_solution(8555570044322217428)
XLA Ops:
  0.6 1.5 %slice_bitcast_fusion = (f32[1,1024]{1,0:T(1,128)}, f32[1,1024]{1,0:T(1,128)}, f32[1,1024]{1,0:T(1,128)}, f32[1,1024]{1,0:T(1,128)}, f32[1,1024]{1,0:T(1,128)}, ...) fusion(f32[2,3,1024]{2,0,1:T(2,128)} %param.8, ...), kind=kLoop, calls=%fused_computation | loop fusion | bytes 98304 | tf_op jit(solution)/shard_map/broadcast_in_dim;squeeze | solution.py:416
  2.1 99.2 %shard_map.77 = (bf16[4,256,1024]{2,1,0:T(8,128)(2,1)}, bf16[4,256,1024]{2,1,0:T(8,128)(2,1)}) custom-call(f32[1,1024]{1,0:T(1,128)} %get-tuple-element.19.refs_0_, f32[1,1024]{1,0:T(1,128)} %get-tuple-element.20.refs_1_, f32[1,1024]{1,0:T(1,128)} %get-tuple-element.21.refs_2_, f32[1,1024]{1,0:T(1,128)} %get-tuple-element.22.refs_3_, ...), custom_call_target="tpu_custom_call" | custom-call | tf_op jit(solution)/shard_map/pallas_call | solution.py:427
  101.4 0.0 copy-start
  101.4 3.2 %copy.10 = bf16[1,4,256,1024]{3,2,1,0:T(8,128)(2,1)} copy(bf16[1,4,256,1024]{3,2,1,0:T(8,128)(2,1)} %bitcast.30) | data formatting | bytes 4194304
  104.6 0.0 copy-done
  104.6 1.3 %copy.11 = bf16[1,4,256,1024]{3,2,1,0:T(8,128)(2,1)} copy(bf16[1,4,256,1024]{3,2,1,0:T(8,128)(2,1)S(1)} %bitcast.29) | data formatting | bytes 4194304
Async XLA Ops:
  101.4 3.2 %copy-start = (bf16[4,256,1024]{2,1,0:T(8,128)(2,1)S(1)}, bf16[4,256,1024]{2,1,0:T(8,128)(2,1)}, u32[]{:S(2)}) copy-start(bf16[4,256,1024]{2,1,0:T(8,128)(2,1)} %get-tuple-element.5) | copy-start | bytes 6291460

commit v7 on v6

--- a/solution.py
+++ b/solution.py
@@ -34,7 +34,7 @@
             placed_ref[j, g] = jnp.where(group == g, moved, 0.0).astype(jnp.bfloat16)
 
 
-def attend(placed_ref, keys_ref, values_ref, mixed_ref, store):
+def attend(placed_ref, keys_ref, values_ref, mixed_ref, store, interlude):
     owners = range(keys_ref.shape[0])
     columns = keys_ref.shape[0] * keys_ref.shape[2]
     width = mixed_ref.shape[1]
@@ -63,6 +63,8 @@
         if first + BUNDLE == KV_HEADS:
             mixed_ref[j] = mixed
         scores = following
+        if index == 3 * len(bundles) // 4:
+            interlude()
     for g in range(KV_HEADS):
         out = jnp.zeros(mixed_ref.shape[1:], jnp.float32)
         group = lane_group(out.shape)
@@ -318,7 +320,7 @@
         kv_start(row)
         mixed_copy(row).start()
 
-    def attend_row(row):
+    def attend_row(row, interlude):
         kv_forward(row)
         place_queries(normed[row], query_weight, placed)
         kv_collect(row)
@@ -326,7 +328,7 @@
         def store(g, value):
             attended[row, :, g * BLOCK : (g + 1) * BLOCK] = value
 
-        attend(placed, keys.at[row], values.at[row], mixed, store)
+        attend(placed, keys.at[row], values.at[row], mixed, store, interlude)
         attended_copy(row).start()
 
     positions = lax.broadcasted_iota(jnp.int32, circle_ref.shape, 0) + (lat * band - 2)
@@ -340,8 +342,9 @@
     loads[1].wait()
     loads[2].wait()
 
-    def one_half(half, carry):
-        def one_stage(stage, carry):
+    def one_stage(stage, carry):
+        @pl.when(stage < band)
+        def _():
             @pl.when(at_pole)
             def _():
                 @pl.when(stage == 0)
@@ -358,18 +361,13 @@
                 def _():
                     halo_copy(stage).wait_send()
 
-            @pl.when(jnp.logical_not(at_pole))
+            @pl.when(jnp.logical_and(stage != 2, jnp.logical_not(at_pole)))
             def _():
                 halo_copy(stage).wait_send()
 
-                @pl.when(stage == 0)
+                @pl.when(stage < 2)
                 def _():
-                    halo_copy(1).start()
-
-                @pl.when(stage == 1)
-                def _():
-                    halo_copy(2).start()
-                    halo_copy(3).start()
+                    halo_copy(stage + 1).start()
 
             halo_arrival(stage).wait_recv()
             for edge in edges(stage):
@@ -381,17 +379,20 @@
             stencil(wide, outer, 1, outer, taps_one, store_after_one, outward)
             stencil(after_one, row + 1, 1, row + 2, taps_two, store_mixed, inner)
             project(row)
-            return carry
-
-        def one_row(stage, carry):
-            attend_row(mixed_row(stage))
-            return carry
-
-        lax.fori_loop(2 * half, 2 * half + 2, one_stage, 0)
-        lax.fori_loop(2 * half, 2 * half + 2, one_row, 0)
+
+        @pl.when(stage > 0)
+        def _():
+            def interlude():
+                @pl.when(jnp.logical_and(stage == 1, jnp.logical_not(at_pole)))
+                def _():
+                    halo_copy(2).wait_send()
+                    halo_copy(3).start()
+
+            attend_row(mixed_row(stage - 1), interlude)
+
         return carry
 
-    lax.fori_loop(0, band // 2, one_half, 0)
+    lax.fori_loop(0, band + 1, one_stage, 0)
 
     for side in sides:
         side.wait_send()

time: 106 us -> 99.9 us (0.942)
  the two profiles are of different devices: /device:TPU:17 before, /device:TPU:25 now
where the time goes in v7:
time: 99.9 us; the launch traced here: 99.6 us
  Pallas kernels  92.9 us (93%)
  local copies, waits for them, and re-layouts  6.04 us (6%)
    pallas_call x1, Pallas kernels, local(): pl.pallas_call(functools.partial(block_kernel, lat_size, lon_size), out_s...  92.9 us
    unnamed x4, local copies, waits for them, and re-layouts  4.55 us

profile of v7, /device:TPU:25, one launch (start us, length us, event | category | flops | bytes accessed | tf_op | source)
XLA Modules:
  0.0 99.6 jit_solution(3999578729192724377)
XLA Ops:
  0.6 1.5 %slice_bitcast_fusion = (f32[1,1024]{1,0:T(1,128)}, f32[1,1024]{1,0:T(1,128)}, f32[1,1024]{1,0:T(1,128)}, f32[1,1024]{1,0:T(1,128)}, f32[1,1024]{1,0:T(1,128)}, ...) fusion(f32[2,3,1024]{2,0,1:T(2,128)} %param.8, ...), kind=kLoop, calls=%fused_computation | loop fusion | bytes 98304 | tf_op jit(solution)/shard_map/broadcast_in_dim;squeeze | solution.py:417
  2.1 92.9 %shard_map.77 = (bf16[4,256,1024]{2,1,0:T(8,128)(2,1)}, bf16[4,256,1024]{2,1,0:T(8,128)(2,1)}) custom-call(f32[1,1024]{1,0:T(1,128)} %get-tuple-element.19.refs_0_, f32[1,1024]{1,0:T(1,128)} %get-tuple-element.20.refs_1_, f32[1,1024]{1,0:T(1,128)} %get-tuple-element.21.refs_2_, f32[1,1024]{1,0:T(1,128)} %get-tuple-element.22.refs_3_, ...), custom_call_target="tpu_custom_call" | custom-call | tf_op jit(solution)/shard_map/pallas_call | solution.py:428
  95.0 0.0 copy-start
  95.0 3.2 %copy.10 = bf16[1,4,256,1024]{3,2,1,0:T(8,128)(2,1)} copy(bf16[1,4,256,1024]{3,2,1,0:T(8,128)(2,1)} %bitcast.30) | data formatting | bytes 4194304
  98.3 0.0 copy-done
  98.3 1.3 %copy.11 = bf16[1,4,256,1024]{3,2,1,0:T(8,128)(2,1)} copy(bf16[1,4,256,1024]{3,2,1,0:T(8,128)(2,1)S(1)} %bitcast.29) | data formatting | bytes 4194304
Async XLA Ops:
  95.0 3.2 %copy-start = (bf16[4,256,1024]{2,1,0:T(8,128)(2,1)S(1)}, bf16[4,256,1024]{2,1,0:T(8,128)(2,1)}, u32[]{:S(2)}) copy-start(bf16[4,256,1024]{2,1,0:T(8,128)(2,1)} %get-tuple-element.5) | copy-start | bytes 6291460
